TPU v7x, 32 devices: a whole 2x2x4 slice. The times are simulated.
32 devices in a mesh: dp: 16 (over z, x, core), tensor: 2 (over y).
Axes of the slice: x: 2, y: 2, z: 4, core: 2. Of those that a mesh axis runs over, the one named last changes fastest.
Arguments:
- patches: bfloat16 [25088, 1024], P('dp'), may hold values from -6 to 6
- cotangent: bfloat16 [25088, 1024], P('dp'), may hold values from -6 to 6
- clip_lengths: int32 [16, 8], P('dp'), may hold values from 0 to 1568, as said below
- attn_gain: float32 [1024], replicated, may hold values from 0.25 to 1.75
- attn_shift: float32 [1024], replicated, may hold values from -3 to 3
- qkv_weight: bfloat16 [1024, 3, 1024], P(None, None, 'tensor'), may hold values from -0.1875 to 0.1875
- qkv_bias: float32 [3, 1024], P(None, 'tensor'), may hold values from -3 to 3
- proj_weight: bfloat16 [1024, 1024], P('tensor'), may hold values from -2 to 2
- proj_bias: float32 [1024], replicated, may hold values from -3 to 3
- mlp_gain: float32 [1024], replicated, may hold values from 0.25 to 1.75
- mlp_shift: float32 [1024], replicated, may hold values from -3 to 3
- up_weight: bfloat16 [1024, 4096], P(None, 'tensor'), may hold values from -0.1875 to 0.1875
- up_bias: float32 [4096], P('tensor'), may hold values from -3 to 3
- down_weight: bfloat16 [4096, 1024], P('tensor'), may hold values from -0.09375 to 0.09375
- down_bias: float32 [1024], replicated, may hold values from -3 to 3
Outputs:
- block_out: bfloat16 [25088, 1024], P('dp')
- patch_grad: bfloat16 [25088, 1024], P('dp')
- attn_gain_grad: float32 [1024], replicated
- attn_shift_grad: float32 [1024], replicated
- qkv_weight_grad: float32 [1024, 3, 1024], P('dp', None, 'tensor')
- qkv_bias_grad: float32 [3, 1024], P(None, 'tensor')
- proj_weight_grad: float32 [1024, 1024], P('tensor', 'dp')
- proj_bias_grad: float32 [1024], replicated
- mlp_gain_grad: float32 [1024], replicated
- mlp_shift_grad: float32 [1024], replicated
- up_weight_grad: float32 [1024, 4096], P('dp', 'tensor')
- up_bias_grad: float32 [4096], P('tensor')
- down_weight_grad: float32 [4096, 1024], P('tensor', 'dp')
- down_bias_grad: float32 [1024], replicated
Inputs may be any that keep to these rules, and one draw needn't show every extreme that they name: `clip_lengths`: each row holds one index of dp: either one video of 1568 tokens followed by zeros, or 8 images of 196 tokens each; every draw has rows of both kinds.
All inputs are finite; a program needn't handle non-finite values.
Results may differ from a plain program's by a relative error of at most 0.015.
Values may be sent and summed in bfloat16 or wider, within the bound.
A program may use at most 448 MiB of HBM per device.

v0:
```python
import jax
import jax.numpy as jnp
from jax import lax
from jax.sharding import PartitionSpec as P

HEAD_DIM = 64
GRID = 14
IMG = 196
QUERY_BLOCK = 784


def layer_norm(values, gain, shift):
    centre = values - jnp.mean(values, axis=-1, keepdims=True)
    spread = jnp.mean(centre * centre, axis=-1, keepdims=True)
    return centre * lax.rsqrt(spread + 1e-06) * gain + shift


def gelu_exact(values):
    return jax.nn.gelu(values, approximate=False)


def rotary_angles(offsets):
    pair_count = HEAD_DIM // 2
    side_pairs = pair_count * 11 // 32
    time_pairs = pair_count - 2 * side_pairs
    pair_index = jnp.arange(pair_count, dtype=jnp.int32)
    time_pair = pair_index < time_pairs
    height_pair = (pair_index >= time_pairs) & (pair_index < time_pairs + side_pairs)
    group_begin = jnp.where(
        time_pair, 0, jnp.where(height_pair, time_pairs, time_pairs + side_pairs)
    )
    group_size = jnp.where(time_pair, time_pairs, side_pairs)
    inverse = jnp.power(
        10000.0, -(pair_index - group_begin).astype(jnp.float32) / group_size.astype(jnp.float32)
    )
    frame_place = (offsets // IMG).astype(jnp.float32)
    row_place = (offsets % IMG // GRID).astype(jnp.float32)
    column_place = (offsets % GRID).astype(jnp.float32)
    position = jnp.where(
        time_pair[None, :],
        frame_place[:, None],
        jnp.where(height_pair[None, :], row_place[:, None], column_place[:, None]),
    )
    angles = position * inverse[None, :]
    angles = jnp.concatenate([angles, angles], axis=1)
    return (jnp.cos(angles), jnp.sin(angles))


def rotate(values, cosine_table, sine_table):
    heads_view = values.reshape(values.shape[0], -1, HEAD_DIM)
    half_dim = HEAD_DIM // 2
    turned = jnp.concatenate([-heads_view[..., half_dim:], heads_view[..., :half_dim]], axis=-1)
    return heads_view * cosine_table[:, None, :] + turned * sine_table[:, None, :]


def unrotate(grad_rows, cosine_table, sine_table):
    half_dim = HEAD_DIM // 2
    turned = jnp.concatenate([-grad_rows[..., half_dim:], grad_rows[..., :half_dim]], axis=-1)
    return grad_rows * cosine_table[:, None, :] - turned * sine_table[:, None, :]


def through(left_side, right_side):
    return lax.dot_general(
        left_side, right_side, (((0,), (0,)), ((), ())), preferred_element_type=jnp.float32
    )


def against(left_side, right_side):
    return lax.dot_general(
        left_side, right_side, (((1,), (1,)), ((), ())), preferred_element_type=jnp.float32
    )


def attend_forward(queries, key_rows, values):
    scaling = HEAD_DIM ** (-0.5)
    scores = (
        jnp.einsum("bqhc,bkhc->bhqk", queries, key_rows, preferred_element_type=jnp.float32)
        * scaling
    )
    row_top = jnp.max(scores, axis=-1, keepdims=True)
    weights = jnp.exp(scores - row_top)
    totals = jnp.sum(weights, axis=-1, keepdims=True)
    softmax_rows = (weights / totals).astype(jnp.bfloat16)
    attended = jnp.einsum(
        "bhqk,bkhc->bqhc", softmax_rows, values, preferred_element_type=jnp.float32
    )
    log_total = (row_top + jnp.log(totals))[..., 0]
    return (attended, jnp.transpose(log_total, (0, 2, 1)))


def attend_backward(queries, key_rows, values, upstream, log_total):
    scaling = HEAD_DIM ** (-0.5)
    scores = (
        jnp.einsum("bqhc,bkhc->bhqk", queries, key_rows, preferred_element_type=jnp.float32)
        * scaling
    )
    softmax_rows = jnp.exp(scores - jnp.transpose(log_total, (0, 2, 1))[..., None])
    value_grad = jnp.einsum(
        "bhqk,bqhc->bkhc",
        softmax_rows.astype(jnp.bfloat16),
        upstream,
        preferred_element_type=jnp.float32,
    )
    prob_grad = jnp.einsum("bqhc,bkhc->bhqk", upstream, values, preferred_element_type=jnp.float32)
    centre = jnp.sum(softmax_rows * prob_grad, axis=-1, keepdims=True)
    score_grad = (softmax_rows * (prob_grad - centre)).astype(jnp.bfloat16)
    query_grad = (
        jnp.einsum("bhqk,bkhc->bqhc", score_grad, key_rows, preferred_element_type=jnp.float32)
        * scaling
    )
    key_grad = (
        jnp.einsum("bhqk,bqhc->bkhc", score_grad, queries, preferred_element_type=jnp.float32)
        * scaling
    )
    return (query_grad, key_grad, value_grad)


def video_forward(queries, key_rows, values):
    tokens = queries.shape[0]
    attended_list = []
    log_list = []
    for block_index in range(tokens // QUERY_BLOCK):
        begin_row = block_index * QUERY_BLOCK
        attended, log_total = attend_forward(
            queries[None, begin_row : begin_row + QUERY_BLOCK], key_rows[None], values[None]
        )
        attended_list.append(attended[0])
        log_list.append(log_total[0])
    return (jnp.concatenate(attended_list, axis=0), jnp.concatenate(log_list, axis=0))


def image_forward(queries, key_rows, values):
    tokens, heads_here, head_dim = queries.shape
    shaped = (tokens // IMG, IMG, heads_here, head_dim)
    attended, log_total = attend_forward(
        queries.reshape(shaped), key_rows.reshape(shaped), values.reshape(shaped)
    )
    return (attended.reshape(tokens, heads_here, head_dim), log_total.reshape(tokens, heads_here))


def video_backward(queries, key_rows, values, upstream, log_total):
    tokens = queries.shape[0]
    query_list = []
    key_total = jnp.zeros(queries.shape, jnp.float32)
    value_total = jnp.zeros(queries.shape, jnp.float32)
    for block_index in range(tokens // QUERY_BLOCK):
        begin_row = block_index * QUERY_BLOCK
        end_row = begin_row + QUERY_BLOCK
        query_grad, key_grad, value_grad = attend_backward(
            queries[None, begin_row:end_row],
            key_rows[None],
            values[None],
            upstream[None, begin_row:end_row],
            log_total[None, begin_row:end_row],
        )
        query_list.append(query_grad[0])
        key_total = key_total + key_grad[0]
        value_total = value_total + value_grad[0]
    return (jnp.concatenate(query_list, axis=0), key_total, value_total)


def image_backward(queries, key_rows, values, upstream, log_total):
    tokens, heads_here, head_dim = queries.shape
    shaped = (tokens // IMG, IMG, heads_here, head_dim)
    query_grad, key_grad, value_grad = attend_backward(
        queries.reshape(shaped),
        key_rows.reshape(shaped),
        values.reshape(shaped),
        upstream.reshape(shaped),
        log_total.reshape(tokens // IMG, IMG, heads_here),
    )
    return (
        query_grad.reshape(queries.shape),
        key_grad.reshape(queries.shape),
        value_grad.reshape(queries.shape),
    )


def on_device(
    patches,
    cotangent,
    clip_lengths,
    attn_gain,
    attn_shift,
    qkv_weight,
    qkv_bias,
    proj_weight,
    proj_bias,
    mlp_gain,
    mlp_shift,
    up_weight,
    up_bias,
    down_weight,
    down_bias,
):
    tokens = patches.shape[0]
    model_width = patches.shape[1]
    local_width = proj_weight.shape[0]
    local_heads = local_width // HEAD_DIM
    clip_len = clip_lengths[0, 0]
    holds_video = clip_len == tokens
    offsets = jnp.arange(tokens, dtype=jnp.int32) % clip_len
    cosine_table, sine_table = rotary_angles(offsets)
    patch_values = patches.astype(jnp.float32)
    normed, first_norm_back = jax.vjp(layer_norm, patch_values, attn_gain, attn_shift)
    normed_low = normed.astype(jnp.bfloat16)
    qkv_flat = qkv_weight.reshape(model_width, 3 * local_width)
    mixed_rows = jnp.dot(
        normed_low, qkv_flat, preferred_element_type=jnp.float32
    ) + qkv_bias.reshape(-1)
    queries = rotate(mixed_rows[:, :local_width], cosine_table, sine_table).astype(jnp.bfloat16)
    key_rows = rotate(
        mixed_rows[:, local_width : 2 * local_width], cosine_table, sine_table
    ).astype(jnp.bfloat16)
    values = (
        mixed_rows[:, 2 * local_width :].reshape(tokens, local_heads, HEAD_DIM).astype(jnp.bfloat16)
    )
    attended, log_total = lax.cond(
        holds_video, video_forward, image_forward, queries, key_rows, values
    )
    attended_low = attended.reshape(tokens, local_width).astype(jnp.bfloat16)
    proj_part = (
        jnp.dot(attended_low, proj_weight, preferred_element_type=jnp.float32)
        .astype(jnp.bfloat16)
        .astype(jnp.float32)
    )
    attn_out = lax.psum(proj_part.astype(jnp.bfloat16), "tensor").astype(jnp.float32)
    residual = patch_values + (attn_out + proj_bias)
    normed_two, second_norm_back = jax.vjp(layer_norm, residual, mlp_gain, mlp_shift)
    normed_two_low = normed_two.astype(jnp.bfloat16)
    upward = jnp.dot(normed_two_low, up_weight, preferred_element_type=jnp.float32) + up_bias
    activated, gelu_back = jax.vjp(gelu_exact, upward)
    activated_low = activated.astype(jnp.bfloat16)
    down_part = (
        jnp.dot(activated_low, down_weight, preferred_element_type=jnp.float32)
        .astype(jnp.bfloat16)
        .astype(jnp.float32)
    )
    mlp_out = lax.psum(down_part.astype(jnp.bfloat16), "tensor").astype(jnp.float32)
    block_out = (residual + (mlp_out + down_bias)).astype(jnp.bfloat16)
    out_grad = cotangent.astype(jnp.float32)
    down_bias_grad = jnp.sum(out_grad, axis=0)
    down_weight_grad = through(activated_low, cotangent)
    activated_grad = against(cotangent, down_weight)
    (upward_grad,) = gelu_back(activated_grad)
    upward_low = upward_grad.astype(jnp.bfloat16)
    up_bias_grad = jnp.sum(upward_low.astype(jnp.float32), axis=0)
    up_weight_grad = through(normed_two_low, upward_low)
    normed_two_part = against(upward_low, up_weight)
    normed_two_grad = lax.psum(normed_two_part.astype(jnp.bfloat16), "tensor").astype(jnp.float32)
    residual_part, mlp_gain_grad, mlp_shift_grad = second_norm_back(normed_two_grad)
    residual_grad = out_grad + residual_part
    branch_low = residual_grad.astype(jnp.bfloat16)
    proj_bias_grad = jnp.sum(branch_low.astype(jnp.float32), axis=0)
    proj_weight_grad = through(attended_low, branch_low)
    attended_grad = (
        against(branch_low, proj_weight).astype(jnp.bfloat16).reshape(tokens, local_heads, HEAD_DIM)
    )
    query_grad, key_grad, value_grad = lax.cond(
        holds_video,
        video_backward,
        image_backward,
        queries,
        key_rows,
        values,
        attended_grad,
        log_total,
    )
    mixed_grad = jnp.concatenate(
        [
            unrotate(query_grad, cosine_table, sine_table).reshape(tokens, local_width),
            unrotate(key_grad, cosine_table, sine_table).reshape(tokens, local_width),
            value_grad.reshape(tokens, local_width),
        ],
        axis=1,
    ).astype(jnp.bfloat16)
    qkv_bias_grad = jnp.sum(mixed_grad.astype(jnp.float32), axis=0).reshape(3, local_width)
    qkv_weight_grad = through(normed_low, mixed_grad).reshape(model_width, 3, local_width)
    normed_part = against(mixed_grad, qkv_flat)
    normed_grad = lax.psum(normed_part.astype(jnp.bfloat16), "tensor").astype(jnp.float32)
    patch_part, attn_gain_grad, attn_shift_grad = first_norm_back(normed_grad)
    patch_grad = (residual_grad + patch_part).astype(jnp.bfloat16)
    qkv_weight_sum, proj_weight_sum, up_weight_sum, down_weight_sum = (
        lax.psum_scatter(qkv_weight_grad, "dp", scatter_dimension=0, tiled=True),
        lax.psum_scatter(proj_weight_grad, "dp", scatter_dimension=1, tiled=True),
        lax.psum_scatter(up_weight_grad, "dp", scatter_dimension=0, tiled=True),
        lax.psum_scatter(down_weight_grad, "dp", scatter_dimension=1, tiled=True),
    )
    (
        attn_gain_sum,
        attn_shift_sum,
        qkv_bias_sum,
        proj_bias_sum,
        mlp_gain_sum,
        mlp_shift_sum,
        up_bias_sum,
        down_bias_sum,
    ) = lax.psum(
        (
            attn_gain_grad,
            attn_shift_grad,
            qkv_bias_grad,
            proj_bias_grad,
            mlp_gain_grad,
            mlp_shift_grad,
            up_bias_grad,
            down_bias_grad,
        ),
        "dp",
    )
    return (
        block_out,
        patch_grad,
        attn_gain_sum,
        attn_shift_sum,
        qkv_weight_sum,
        qkv_bias_sum,
        proj_weight_sum,
        proj_bias_sum,
        mlp_gain_sum,
        mlp_shift_sum,
        up_weight_sum,
        up_bias_sum,
        down_weight_sum,
        down_bias_sum,
    )


def solution(mesh):
    return jax.shard_map(
        on_device,
        mesh=mesh,
        in_specs=(
            P("dp", None),
            P("dp", None),
            P("dp", None),
            P(),
            P(),
            P(None, None, "tensor"),
            P(None, "tensor"),
            P("tensor", None),
            P(),
            P(),
            P(),
            P(None, "tensor"),
            P("tensor"),
            P("tensor", None),
            P(),
        ),
        out_specs=(
            P("dp", None),
            P("dp", None),
            P(),
            P(),
            P("dp", None, "tensor"),
            P(None, "tensor"),
            P("tensor", "dp"),
            P(),
            P(),
            P(),
            P("dp", "tensor"),
            P("tensor"),
            P("tensor", "dp"),
            P(),
        ),
        check_vma=False,
    )
```

profile of v0, /device:TPU:0, one launch (start us, length us, event | category | flops | bytes accessed | tf_op | source)
XLA Modules:
  0.0 1350.0 jit_solution(14208614494212649916)
XLA Ops:
  12.1 2.9 fusion.63
  15.6 4.7 copy.96
  20.3 8.5 convolution_add_fusion
  30.2 3.5 fusion.112
  36.1 2.7 copy.99
  38.9 5.2 copy.98
  44.0 4.6 copy.97
  48.6 3.8 slice_negate_fusion
  56.0 61.5 %conditional.4 = (f32[1568,8]{0,1:T(8,128)S(1)}, bf16[1568,512]{0,1:T(8,128)(2,1)}) conditional(s32[]{:T(128)} %convert_element_type.160, (bf16[1568,8,64]{0,2,1:T(8,128)(2,1)}, bf16[1568,8,64]{0,2,1:T(8,128)(2,1)}, bf16[1568,8,64]{0,2,1:T(8,128)(2,1)S(1)}) %tuple.103, (bf16[1568,8,64]{0,2,1:T(8,128)(2,1)}, bf16[1568,8,64]{0,2,1:T(8,128)(2,1)}, ...), branch_computations={%region_2.5_spmd, %region_5.10_spmd} | conditional | flops 5215494144 | bytes 249800720
  56.1 5.6 reshape.522
  61.8 5.6 reshape.523
  67.4 4.3 reshape.525
  71.7 4.9 multiply_reduce_fusion
  76.5 4.7 copy-done.9
  81.2 3.3 fusion
  84.5 9.5 convert_bitcast_fusion
  94.2 2.9 copy.81
  97.1 3.5 reshape.548
  117.5 5.0 convolution_convert_fusion.3
  122.6 142.1 %all-reduce.8.cloned.1.call-done = bf16[1568,1024]{1,0:T(8,128)(2,1)} async-done(((bf16[1568,1024]{1,0:T(8,128)(2,1)}), bf16[1568,1024]{1,0:T(8,128)(2,1)}) %all-reduce.8.cloned.1.call-update) | async-done | bytes 3211280 | tf_op jit(solution)/shard_map/psum | solution.py:227
  264.8 4.2 fusion.68
  271.8 10.0 fusion.103
  281.8 41.7 %convert_reduce_fusion = (f32[2048]{0:T(1024)}, bf16[1568,2048]{1,0:T(8,128)(2,1)S(1)}, f32[1568,2048]{1,0:T(8,128)}) fusion(f32[1568,2048]{1,0:T(8,128)S(1)} %fusion.103, f32[2048]{0:T(1024)S(1)} %copy-done.62, bf16[1568,1024]{1,0:T(8,128)(2,1)S(1)} %copy-done.20, bf16[2048,1024]{1,0:T(8,128)(2,1)} %param.32), kind=kOutput, calls=%fused_computation.74 | convolution fusion | flops 6817511424 | bytes 39534592 | tf_op jit(solution)/shard_map/dot_general | solution.py:69
  323.5 2.8 copy-done.72
  326.3 8.4 convolution_convert_fusion.1
  334.8 13.1 multiply_convert_fusion.3
  347.9 74.2 %all-reduce.10.cloned.1.call-done = bf16[1568,1024]{1,0:T(8,128)(2,1)} async-done(((bf16[1568,1024]{1,0:T(8,128)(2,1)}), bf16[1568,1024]{1,0:T(8,128)(2,1)}) %all-reduce.10.cloned.1.call-update) | async-done | bytes 3211280 | tf_op jit(solution)/shard_map/psum | solution.py:250
  422.1 6.2 convert_reduce_fusion.3
  428.7 4.4 fusion.65
  433.2 4.5 convert_reduce_fusion.6
  437.7 3.1 convolution_convert_fusion.4
  440.8 106.6 %conditional.10 = (f32[1568,8,64]{0,2,1:T(8,128)}, f32[1568,8,64]{0,2,1:T(8,128)}, bf16[1568,512]{0,1:T(8,128)(2,1)}) conditional(s32[]{:T(128)} %convert_element_type.160, (bf16[1568,8,64]{0,2,1:T(8,128)(2,1)}, bf16[1568,8,64]{0,2,1:T(8,128)(2,1)}, f32[1568,8]{0,1:T(8,128)S(1)}, bf16[1568,512]{1,0:T(8,128)(2,1)}, ...), branch_computations={%region_17.19_spmd, %region_19.22_spmd} | conditional | flops 12828987392 | bytes 646470656 | solution.py:259
  441.0 4.5 reshape.530
  445.4 5.8 reshape.528
  451.2 5.6 reshape.527
  456.8 3.0 reshape.553
  459.8 4.8 copy.85
  464.6 4.1 fusion.21
  468.8 11.2 multiply_reduce_fusion.3
  479.9 8.6 multiply_convert_fusion
  488.5 7.5 convert_bitcast_fusion.1
  496.0 2.6 copy.95
  498.6 4.7 reshape.549
  503.4 7.8 multiply_bitcast_fusion
  512.3 4.4 copy.89
  516.7 5.4 reshape.531
  522.1 6.6 copy.92
  528.7 5.4 reshape.532
  554.6 8.8 fusion.101
  563.4 9.5 copy.103
  573.2 11.4 convolution_convert_fusion.2
  584.6 6.9 convolution_convert_fusion
  591.6 5.9 fusion.113
  597.6 13.0 fusion.114
  611.4 14.7 %fusion.102 = f32[1024,2048]{1,0:T(8,128)} fusion(bf16[1568,2048]{1,0:T(8,128)(2,1)} %copy-done.72, f32[1024]{0:T(1024)S(1)} %copy-done.70, f32[1024]{0:T(1024)S(1)} %copy-done.56, f32[1568]{0:T(1024)S(1)} %copy-done.46, bf16[1568,1024]{1,0:T(8,128)(2,1)} %all-reduce.8.cloned.1.call-done, bf16[1568,1024]{1,0:T(8,128)(2,1)} %param.19, ...), kind=kOutput, calls=%fused_computation.198 | convolution fusion | flops 6591119360 | bytes 21258496 | tf_op jit(solution)/shard_map/dot_general | solution.py:63
  627.9 2.8 convert_reduce_fusion.1
  630.7 268.4 %all-reduce.12.cloned.1.call-done = f32[1024,3,512]{2,1,0:T(4,128)} async-done(((f32[1024,3,512]{2,1,0:T(4,128)}), f32[1024,3,512]{2,1,0:T(4,128)}) %all-reduce.12.cloned.1.call-update) | async-done | bytes 6291472
  901.1 157.4 %all-reduce.14.cloned.1.call-done = (bf16[1568,1024]{1,0:T(8,128)(2,1)}, bf16[1568,1024]{1,0:T(8,128)(2,1)}) async-done(((bf16[1568,1024]{1,0:T(8,128)(2,1)}, bf16[1568,1024]{1,0:T(8,128)(2,1)}), (bf16[1568,1024]{1,0:T(8,128)(2,1)}, bf16[1568,1024]{1,0:T(8,128)(2,1)})) %all-reduce.14.cloned.1.call-update) | async-done | bytes 6422544 | tf_op jit(solution)/shard_map/psum | solution.py:239
  1058.5 5.0 convert_reduce_fusion.2
  1063.5 6.0 fusion.66
  1069.6 10.9 add_convert_fusion.2
  1080.6 62.1 %all-reduce.1 = (f32[1024]{0:T(1024)}, f32[1024]{0:T(1024)}, f32[3,512]{1,0:T(4,128)}, f32[1024]{0:T(1024)}, f32[1024]{0:T(1024)}, /*index=5*/f32[1024]{0:T(1024)}, f32[2048]{0:T(1024)}, f32[1024]{0:T(1024)}) all-reduce(f32[1024]{0:T(1024)S(1)} %get-tuple-element.150, ...), channel_id=1, replica_groups=mesh['dp'=16,'tensor'=2] {'dp'}, use_global_device_ids=true, to_apply=%region_26.27 | all-reduce | flops 9728 | bytes 77824 | tf_op jit(solution)/shard_map/psum | solution.py:298
  1142.7 90.4 %reduce-scatter.8.cloned.1.call-done = f32[2048,64]{0,1:T(8,128)} async-done(((f32[2048,1024]{0,1:T(8,128)}), f32[2048,64]{0,1:T(8,128)}) %reduce-scatter.8.cloned.1.call-update) | async-done | bytes 524304 | tf_op jit(solution)/shard_map/reduce_scatter | solution.py:287
  1233.1 109.7 %reduce-scatter.6.cloned.1.call-done = f32[64,2048]{1,0:T(8,128)} async-done(((f32[1024,2048]{1,0:T(8,128)}), f32[64,2048]{1,0:T(8,128)}) %reduce-scatter.6.cloned.1.call-update) | async-done | bytes 524304 | tf_op jit(solution)/shard_map/reduce_scatter | solution.py:286
  (194 shorter events, 27.8 us)
Async XLA Ops:
  7.2 110.3 %copy-start = (bf16[512,1024]{1,0:T(8,128)(2,1)S(1)}, bf16[512,1024]{1,0:T(8,128)(2,1)}, u32[]{:S(2)}) copy-start(bf16[512,1024]{1,0:T(8,128)(2,1)} %param.26) | copy-start | bytes 3145732
  7.2 13.1 copy-start.57
  7.2 13.1 copy-start.67
  7.2 257.6 %all-reduce.8.cloned.1.call-start = ((), (), s32[]{:S(2)}) async-start(), calls=%async_computation.3 | async-start | bytes 6422528 | tf_op jit(solution)/shard_map/psum | solution.py:227
  12.1 16.7 %copy-start.39 = (f32[1568]{0:T(1024)}, f32[1568]{0:T(1024)S(1)}, u32[]{:S(2)}) copy-start(f32[1568]{0:T(1024)S(1)} %broadcast_multiply_fusion.1) | copy-start | bytes 18820
  15.6 13.1 copy-start.47
  30.2 3.5 copy-start.65
  38.9 17.1 %copy-start.12 = (bf16[1568,512]{0,1:T(8,128)(2,1)}, bf16[1568,512]{0,1:T(8,128)(2,1)S(1)}, u32[]{:S(2)}) copy-start(bf16[1568,512]{0,1:T(8,128)(2,1)S(1)} %copy.99) | copy-start | bytes 4816900
  48.6 4.0 copy-start.14
  48.6 5.0 copy-start.15
  48.6 5.0 copy-start.29
  48.6 5.1 copy-start.31
  76.5 4.7 copy-start.9
  117.5 5.1 copy-start.35
  117.5 147.3 %copy-start.41 = (f32[1024]{0:T(1024)S(1)}, f32[1024]{0:T(1024)}, u32[]{:S(2)}) copy-start(f32[1024]{0:T(1024)} %param.27) | copy-start | bytes 12292
  122.6 149.2 %copy-start.55 = (f32[1024]{0:T(1024)S(1)}, f32[1024]{0:T(1024)}, u32[]{:S(2)}) copy-start(f32[1024]{0:T(1024)} %param.28) | copy-start | bytes 12292
  122.6 149.2 %copy-start.69 = (f32[1024]{0:T(1024)S(1)}, f32[1024]{0:T(1024)}, u32[]{:S(2)}) copy-start(f32[1024]{0:T(1024)} %param.29) | copy-start | bytes 12292
  122.6 299.5 %all-reduce.10.cloned.1.call-start = ((), (), s32[]{:S(2)}) async-start(), calls=%async_computation.4 | async-start | bytes 6422528 | tf_op jit(solution)/shard_map/psum | solution.py:250
  264.8 4.2 copy-start.2
  264.8 4.8 copy-start.6
  269.5 163.6 %copy-start.37 = (f32[1568]{0:T(1024)}, f32[1568]{0:T(1024)S(1)}, u32[]{:S(2)}) copy-start(f32[1568]{0:T(1024)S(1)} %broadcast_multiply_fusion) | copy-start | bytes 18820
  271.8 161.4 %copy-start.45 = (f32[1568]{0:T(1024)}, f32[1568]{0:T(1024)S(1)}, u32[]{:S(2)}) copy-start(f32[1568]{0:T(1024)S(1)} %fusion.99) | copy-start | bytes 18820
  271.8 10.0 copy-start.20
  271.8 10.0 copy-start.62
  281.8 41.7 %copy-start.22 = (f32[1568,2048]{1,0:T(8,128)}, f32[1568,2048]{1,0:T(8,128)S(1)}, u32[]{:S(2)}) copy-start(f32[1568,2048]{1,0:T(8,128)S(1)} %fusion.103) | copy-start | bytes 38535172
  281.8 44.5 %copy-start.66 = (bf16[1024,2048]{1,0:T(8,128)(2,1)S(1)}, bf16[1024,2048]{1,0:T(8,128)(2,1)}, u32[]{:S(2)}) copy-start(bf16[1024,2048]{1,0:T(8,128)(2,1)} %param.30) | copy-start | bytes 12582916
  334.8 564.3 %all-reduce.12.cloned.1.call-start = ((), (), s32[]{:S(2)}) async-start(), calls=%async_computation.8 | async-start | bytes 16777216
  347.9 80.5 %copy-start.54 = (f32[1568]{0:T(1024)S(1)}, f32[1568]{0:T(1024)}, u32[]{:S(2)}) copy-start(f32[1568]{0:T(1024)} %copy-done.53) | copy-start | bytes 18820
  422.1 6.2 copy-start.3
  422.1 6.2 copy-start.7
  422.1 6.6 copy-start.10
  428.3 4.9 copy-start.21
  428.7 8.9 copy-start.43
  433.2 4.5 copy-start.49
  437.7 3.1 copy-start.33
  437.7 3.1 copy-start.13
  445.4 11.4 copy-start.28
  498.6 12.5 slice-start
  503.4 7.8 slice-start.1
  503.4 7.8 copy-start.19
  547.5 4.0 copy-start.16
  547.5 4.0 copy-start.30
  547.5 4.1 copy-start.32
  552.8 10.6 copy-start.24
  572.9 485.5 %all-reduce.14.cloned.1.call-start = ((), (), s32[]{:S(2)}) async-start(), calls=%async_computation.9 | async-start | bytes 12845056 | tf_op jit(solution)/shard_map/psum | solution.py:239
  573.2 11.5 copy-start.25
  573.2 11.5 copy-start.27
  573.2 11.5 copy-start.34
  591.6 551.1 %reduce-scatter.4.cloned.1.call-start = ((), (), s32[]{:S(2)}) async-start(), calls=%async_computation.5 | async-start | bytes 2228224 | tf_op jit(solution)/shard_map/reduce_scatter | solution.py:285
  597.6 635.6 %reduce-scatter.8.cloned.1.call-start = ((), (), s32[]{:S(2)}) async-start(), calls=%async_computation.7 | async-start | bytes 8912896 | tf_op jit(solution)/shard_map/reduce_scatter | solution.py:287
  610.7 732.1 %reduce-scatter.6.cloned.1.call-start = ((), (), s32[]{:S(2)}) async-start(), calls=%async_computation.6 | async-start | bytes 8912896 | tf_op jit(solution)/shard_map/reduce_scatter | solution.py:286
  627.9 435.6 %copy-start.52 = (f32[1568]{0:T(1024)S(1)}, f32[1568]{0:T(1024)}, u32[]{:S(2)}) copy-start(f32[1568]{0:T(1024)} %copy-done.51) | copy-start | bytes 18820
  1058.5 5.1 copy-start.18
  1058.5 11.0 copy-start.5
  1058.5 11.0 copy-start.8
  1058.5 11.1 copy-start.11
  1058.5 11.1 copy-start.44
  1058.5 11.1 copy-start.50
  1058.5 11.1 copy-start.64
  1069.6 11.0 copy-start.59
  1069.6 11.0 copy-start.60
  1069.6 11.0 copy-start.61
  1069.6 11.0 copy-start.63
  1069.6 273.2 %copy-start.1 = (bf16[512,1024]{1,0:T(8,128)(2,1)S(1)}, bf16[512,1024]{1,0:T(8,128)(2,1)}, u32[]{:S(2)}) copy-start(bf16[512,1024]{1,0:T(8,128)(2,1)} %param.26) | copy-start | bytes 3145732
  (17 other events, 31.3 us)
Sparse Core Ops, SparseCore 0:
  122.7 142.0 all-reduce.7
  334.9 87.1 all-reduce.9
  573.1 326.0 all-reduce.11
  902.2 156.2 all-reduce.13
  1062.6 61.7 reduce-scatter.3
  1129.4 103.6 reduce-scatter.7
  1238.3 104.4 reduce-scatter.5
where the time goes:
time: 1360 us; the launch traced here: 1350 us
  waiting for transfers between devices  842 us (62%)
  matrix products  184 us (14%)
  local copies, waits for them, and re-layouts  125 us (9%)
  other arithmetic  88.4 us (6%)
  blocking collectives  62.1 us (5%)
  loops' own time  30.5 us (2%)
  between operations  17.2 us (1%)
    unnamed x8, waiting for transfers between devices  269 us
    psum x1, waiting for transfers between devices, on_device(): lax.psum(down_part.astype(jnp.bfloat16), 'tensor').astype(jnp.float32)  157 us
    psum x1, waiting for transfers between devices, on_device(): lax.psum(proj_part.astype(jnp.bfloat16), 'tensor').astype(jnp.float32)  142 us
    reduce_scatter x1, waiting for transfers between devices, on_device(): lax.psum_scatter(up_weight_grad, 'dp', scatter_dimension=0, tiled=True)  110 us
    reduce_scatter x1, waiting for transfers between devices, on_device(): lax.psum_scatter(down_weight_grad, 'dp', scatter_dimension=1, tiled=True)  90.4 us
    psum x1, waiting for transfers between devices, on_device(): lax.psum(normed_two_part.astype(jnp.bfloat16), 'tensor').astype(jnp.float32)  74.2 us
    psum x1, blocking collectives, on_device(): lax.psum((attn_gain_grad, attn_shift_grad, qkv_bias_grad, proj_bias_grad,...  62.1 us
    dot_general x4, matrix products, against(): lax.dot_general(left_side, right_side, (((1,), (1,)), ((), ())), preferre...  60.1 us
  transfers between devices with their start and end apart: 7, of which 6 were waited for; matrix products, arithmetic and copies ran while one was open for 7% of the time, Pallas kernels for 0%

commit v1 on v0

v1 whole, which is shorter than its diff:
```python
import functools
import math

import jax
import jax.numpy as jnp
from jax import lax
from jax.experimental import pallas as pl
from jax.experimental.pallas import tpu as pltpu
from jax.sharding import PartitionSpec as P

HEAD_DIM = 64
HALF_DIM = HEAD_DIM // 2
GRID = 14
IMG = 196
EPS = 1e-06
SCALING = HEAD_DIM ** (-0.5)
LOG2E = math.log2(math.e)
TILE = 256
FF_TILE = 512
FWD_CALLS = 4
BWD_CALLS = 4
VMEM_LIMIT = 60 * 1024 * 1024

bf16 = jnp.bfloat16
f32 = jnp.float32


def dot(left, right, left_dim, right_dim):
    return lax.dot_general(
        left, right, (((left_dim,), (right_dim,)), ((), ())), preferred_element_type=f32
    )


def rotary_angles(offsets):
    pair_count = HALF_DIM
    side_pairs = pair_count * 11 // 32
    time_pairs = pair_count - 2 * side_pairs
    pair_index = jnp.arange(pair_count, dtype=jnp.int32)
    time_pair = pair_index < time_pairs
    height_pair = (pair_index >= time_pairs) & (pair_index < time_pairs + side_pairs)
    group_begin = jnp.where(
        time_pair, 0, jnp.where(height_pair, time_pairs, time_pairs + side_pairs)
    )
    group_size = jnp.where(time_pair, time_pairs, side_pairs)
    inverse = jnp.power(
        10000.0, -(pair_index - group_begin).astype(f32) / group_size.astype(f32)
    )
    frame_place = (offsets // IMG).astype(f32)
    row_place = (offsets % IMG // GRID).astype(f32)
    column_place = (offsets % GRID).astype(f32)
    position = jnp.where(
        time_pair[:, None],
        frame_place[None, :],
        jnp.where(height_pair[:, None], row_place[None, :], column_place[None, :]),
    )
    angles = position * inverse[:, None]
    return (jnp.cos(angles), jnp.sin(angles))


def qkv_kernel(x_ref, gain_ref, shift_ref, w_ref, b_ref, cos_ref, sin_ref, normed_ref, out_ref):
    part = pl.program_id(0)

    @pl.when(part == 0)
    def _():
        x = x_ref[...].astype(f32)
        centre = x - jnp.mean(x, axis=1, keepdims=True)
        spread = jnp.mean(centre * centre, axis=1, keepdims=True)
        y = centre * lax.rsqrt(spread + EPS) * gain_ref[...] + shift_ref[...]
        normed_ref[...] = y.astype(bf16)

    mixed = dot(w_ref[...], normed_ref[...], 0, 1) + b_ref[...]
    cosine, sine = cos_ref[...], sin_ref[...]
    for begin in range(0, out_ref.shape[0], HEAD_DIM):
        low = mixed[begin : begin + HALF_DIM]
        high = mixed[begin + HALF_DIM : begin + HEAD_DIM]

        @pl.when(part < 2)
        def _():
            out_ref[begin : begin + HALF_DIM, :] = (low * cosine - high * sine).astype(bf16)
            out_ref[begin + HALF_DIM : begin + HEAD_DIM, :] = (high * cosine + low * sine).astype(
                bf16
            )

        @pl.when(part == 2)
        def _():
            out_ref[begin : begin + HALF_DIM, :] = low.astype(bf16)
            out_ref[begin + HALF_DIM : begin + HEAD_DIM, :] = high.astype(bf16)


def qkv_forward(patches, gain, shift, weight, bias, cosine, sine):
    tokens, width = patches.shape
    columns = weight.shape[1]
    part = columns // 3
    whole = lambda i: (0, 0)
    return pl.pallas_call(
        qkv_kernel,
        grid=(3,),
        out_shape=(
            jax.ShapeDtypeStruct((tokens, width), bf16),
            jax.ShapeDtypeStruct((columns, tokens), bf16),
        ),
        in_specs=[
            pl.BlockSpec((tokens, width), whole),
            pl.BlockSpec((1, width), whole),
            pl.BlockSpec((1, width), whole),
            pl.BlockSpec((width, part), lambda i: (0, i)),
            pl.BlockSpec((part, 1), lambda i: (i, 0)),
            pl.BlockSpec(cosine.shape, whole),
            pl.BlockSpec(sine.shape, whole),
        ],
        out_specs=(
            pl.BlockSpec((tokens, width), whole),
            pl.BlockSpec((part, tokens), lambda i: (i, 0)),
        ),
        compiler_params=pltpu.CompilerParams(vmem_limit_bytes=VMEM_LIMIT),
        cost_estimate=pl.CostEstimate(
            flops=2 * tokens * width * columns, bytes_accessed=14_000_000, transcendentals=0
        ),
        name="qkv_forward",
    )(patches, gain[None, :], shift[None, :], weight, bias[:, None], cosine, sine)


def query_tiles(tokens):
    return [(begin, min(begin + TILE, tokens)) for begin in range(0, tokens, TILE)]


def key_window(begin, end, tokens):
    low = begin // IMG * IMG // 128 * 128
    high = min(tokens, ((end - 1) // IMG + 1) * IMG)
    return low, min(tokens, (high + 127) // 128 * 128)


def attend_kernel(len_ref, q_ref, k_ref, v_ref, e_ref, half_ref, whole_ref, total_ref, out_scr):
    tokens = q_ref.shape[1]
    half = tokens // 2
    holds_video = len_ref[0, 0] == tokens

    def one_tile(begin, end, low, high, masked):
        scores = dot(k_ref[:, low:high], q_ref[:, begin:end], 0, 0)
        if masked:
            width = end - begin
            query = begin + lax.broadcasted_iota(jnp.int32, (1, width), 1)
            first = jnp.zeros((1, width), jnp.int32)
            for clip in range(1, tokens // IMG):
                first = jnp.where(query >= clip * IMG, clip * IMG, first)
            key = low + lax.broadcasted_iota(jnp.int32, (high - low, width), 0)
            scores = jnp.where((key >= first) & (key < first + IMG), scores, -1e30)
        top = jnp.max(scores, axis=0, keepdims=True)
        weights = jnp.exp2((scores - top) * (SCALING * LOG2E))
        weights_low = weights.astype(bf16)
        e_ref[0, low:high, begin:end] = weights_low
        if low > 0:
            e_ref[0, :low, begin:end] = jnp.zeros((low, end - begin), bf16)
        if high < tokens:
            e_ref[0, high:, begin:end] = jnp.zeros((tokens - high, end - begin), bf16)
        total = jnp.sum(weights, axis=0, keepdims=True)
        out = dot(v_ref[:, low:high], weights_low, 1, 0)
        out_scr[:, begin:end] = out / total
        total_ref[0, :, begin:end] = total

    @pl.when(holds_video)
    def _():
        for begin, end in query_tiles(tokens):
            one_tile(begin, end, 0, tokens, False)

    @pl.when(jnp.logical_not(holds_video))
    def _():
        for begin, end in query_tiles(tokens):
            low, high = key_window(begin, end, tokens)
            one_tile(begin, end, low, high, True)

    out = out_scr[...].astype(bf16)
    whole_ref[...] = out
    half_ref[0] = out[:, :half]
    half_ref[1] = out[:, half:]


def attend_forward(qkv, clip_lengths, first_head, heads):
    columns, tokens = qkv.shape
    local_heads = columns // 3 // HEAD_DIM
    half = tokens // 2
    block = lambda part: pl.BlockSpec(
        (HEAD_DIM, tokens), lambda i: (part * local_heads + first_head + i, 0)
    )
    return pl.pallas_call(
        attend_kernel,
        grid=(heads,),
        out_shape=(
            jax.ShapeDtypeStruct((heads, tokens, tokens), bf16),
            jax.ShapeDtypeStruct((2, heads * HEAD_DIM, half), bf16),
            jax.ShapeDtypeStruct((heads * HEAD_DIM, tokens), bf16),
            jax.ShapeDtypeStruct((heads, 1, tokens), f32),
        ),
        in_specs=[pl.BlockSpec(memory_space=pltpu.SMEM), block(0), block(1), block(2)],
        out_specs=(
            pl.BlockSpec((1, tokens, tokens), lambda i: (i, 0, 0)),
            pl.BlockSpec((2, HEAD_DIM, half), lambda i: (0, i, 0)),
            pl.BlockSpec((HEAD_DIM, tokens), lambda i: (i, 0)),
            pl.BlockSpec((1, 1, tokens), lambda i: (i, 0, 0)),
        ),
        scratch_shapes=[pltpu.VMEM((HEAD_DIM, tokens), f32)],
        compiler_params=pltpu.CompilerParams(vmem_limit_bytes=VMEM_LIMIT),
        cost_estimate=pl.CostEstimate(
            flops=16 * heads * tokens * tokens * HEAD_DIM,
            bytes_accessed=2 * heads * tokens * tokens,
            transcendentals=heads * tokens * tokens,
        ),
        name="attend_forward",
    )(clip_lengths, qkv, qkv, qkv)


def attend_back_kernel(
    e_ref,
    q_ref,
    k_ref,
    v_ref,
    out_ref,
    total_ref,
    left_ref,
    right_ref,
    cos_ref,
    sin_ref,
    half_ref,
    whole_ref,
    up_scr,
    up_low,
    score_grad,
):
    tokens = q_ref.shape[1]
    half = tokens // 2
    up_scr[:, :half] = left_ref[...].astype(f32)
    up_scr[:, half:] = right_ref[...].astype(f32)
    up_low[...] = (up_scr[...] / total_ref[0]).astype(bf16)
    centre = jnp.sum(up_low[...].astype(f32) * out_ref[...].astype(f32), axis=0, keepdims=True)
    for begin, end in query_tiles(tokens):
        prob_grad = dot(v_ref[...], up_low[:, begin:end], 0, 0)
        score_grad[:, begin:end] = (
            e_ref[0, :, begin:end].astype(f32) * (prob_grad - centre[:, begin:end])
        ).astype(bf16)
    cosine, sine = cos_ref[...], sin_ref[...]

    def store(part, low, high):
        for row, value in ((0, low), (HALF_DIM, high)):
            value = value.astype(bf16)
            whole_ref[part, row : row + HALF_DIM] = value
            half_ref[0, part, row : row + HALF_DIM] = value[:, :half]
            half_ref[1, part, row : row + HALF_DIM] = value[:, half:]

    def unrotated(part, grad):
        low, high = grad[:HALF_DIM] * SCALING, grad[HALF_DIM:] * SCALING
        store(part, low * cosine + high * sine, high * cosine - low * sine)

    value_grad = dot(up_low[...], e_ref[0], 1, 1)
    store(2, value_grad[:HALF_DIM], value_grad[HALF_DIM:])
    unrotated(1, dot(q_ref[...], score_grad[...], 1, 1))
    unrotated(0, dot(k_ref[...], score_grad[...], 1, 0))


def attend_backward(weights, qkv, attended, totals, left, right, cosine, sine, first, inner, heads):
    columns, tokens = qkv.shape
    local_heads = columns // 3 // HEAD_DIM
    half = tokens // 2
    block = lambda part: pl.BlockSpec(
        (HEAD_DIM, tokens), lambda i: (part * local_heads + first + i, 0)
    )
    whole = lambda i: (0, 0)
    return pl.pallas_call(
        attend_back_kernel,
        grid=(heads,),
        out_shape=(
            jax.ShapeDtypeStruct((2, 3, heads * HEAD_DIM, half), bf16),
            jax.ShapeDtypeStruct((3, heads * HEAD_DIM, tokens), bf16),
        ),
        in_specs=[
            pl.BlockSpec((1, tokens, tokens), lambda i: (inner + i, 0, 0)),
            block(0),
            block(1),
            block(2),
            pl.BlockSpec((HEAD_DIM, tokens), lambda i: (inner + i, 0)),
            pl.BlockSpec((1, 1, tokens), lambda i: (inner + i, 0, 0)),
            pl.BlockSpec((HEAD_DIM, half), lambda i: (first + i, 0)),
            pl.BlockSpec((HEAD_DIM, half), lambda i: (first + i, 0)),
            pl.BlockSpec(cosine.shape, whole),
            pl.BlockSpec(sine.shape, whole),
        ],
        out_specs=(
            pl.BlockSpec((2, 3, HEAD_DIM, half), lambda i: (0, 0, i, 0)),
            pl.BlockSpec((3, HEAD_DIM, tokens), lambda i: (0, i, 0)),
        ),
        scratch_shapes=[
            pltpu.VMEM((HEAD_DIM, tokens), f32),
            pltpu.VMEM((HEAD_DIM, tokens), bf16),
            pltpu.VMEM((tokens, tokens), bf16),
        ],
        compiler_params=pltpu.CompilerParams(vmem_limit_bytes=VMEM_LIMIT),
        cost_estimate=pl.CostEstimate(
            flops=32 * heads * tokens * tokens * HEAD_DIM,
            bytes_accessed=2 * heads * tokens * tokens,
            transcendentals=0,
        ),
        name="attend_backward",
    )(weights, qkv, qkv, qkv, attended, totals, left, right, cosine, sine)


def normal_parts(value):
    a = jnp.abs(value)
    t = 1.0 / (1.0 + (0.3275911 / math.sqrt(2.0)) * a)
    bell = jnp.exp2(value * value * (-0.5 * LOG2E))
    c = [0.5 * x for x in (0.254829592, -0.284496736, 1.421413741, -1.453152027, 1.061405429)]
    tail = ((((c[4] * t + c[3]) * t + c[2]) * t + c[1]) * t + c[0]) * t * bell
    return jnp.where(value >= 0, 1.0 - tail, tail), bell * (1.0 / math.sqrt(2.0 * math.pi))


def mlp_kernel(n_ref, c_ref, up_ref, bias_ref, down_ref, out_ref, ngrad_ref, w_ref, bgrad_ref):
    step = pl.program_id(0)
    upward = dot(n_ref[...], up_ref[...], 1, 0) + bias_ref[...]
    act_grad = dot(c_ref[...], down_ref[...], 1, 1)
    share, density = normal_parts(upward)
    activated = (upward * share).astype(bf16)
    upward_grad = (act_grad * (share + upward * density)).astype(bf16)
    bgrad_ref[...] = jnp.sum(upward_grad.astype(f32), axis=0, keepdims=True)
    out = dot(activated, down_ref[...], 1, 0)
    ngrad = dot(upward_grad, up_ref[...], 1, 1)

    @pl.when(step == 0)
    def _():
        out_ref[...] = out
        ngrad_ref[...] = ngrad

    @pl.when(step > 0)
    def _():
        out_ref[...] += out
        ngrad_ref[...] += ngrad

    w_ref[0] = dot(n_ref[...], upward_grad, 0, 0).astype(bf16)
    w_ref[1] = dot(c_ref[...], activated, 0, 0).astype(bf16)


def mlp(normed, cotangent, up_weight, up_bias, down_weight):
    tokens, width = normed.shape
    hidden = up_weight.shape[1]
    whole = lambda i: (0, 0)
    return pl.pallas_call(
        mlp_kernel,
        grid=(hidden // FF_TILE,),
        out_shape=(
            jax.ShapeDtypeStruct((tokens, width), f32),
            jax.ShapeDtypeStruct((tokens, width), f32),
            jax.ShapeDtypeStruct((2, width, hidden), bf16),
            jax.ShapeDtypeStruct((1, hidden), f32),
        ),
        in_specs=[
            pl.BlockSpec((tokens, width), whole),
            pl.BlockSpec((tokens, width), whole),
            pl.BlockSpec((width, FF_TILE), lambda i: (0, i)),
            pl.BlockSpec((1, FF_TILE), lambda i: (0, i)),
            pl.BlockSpec((FF_TILE, width), lambda i: (i, 0)),
        ],
        out_specs=(
            pl.BlockSpec((tokens, width), whole),
            pl.BlockSpec((tokens, width), whole),
            pl.BlockSpec((2, width, FF_TILE), lambda i: (0, 0, i)),
            pl.BlockSpec((1, FF_TILE), lambda i: (0, i)),
        ),
        compiler_params=pltpu.CompilerParams(vmem_limit_bytes=VMEM_LIMIT),
        cost_estimate=pl.CostEstimate(
            flops=12 * tokens * width * hidden,
            bytes_accessed=24_000_000,
            transcendentals=tokens * hidden,
        ),
        name="feed_forward",
    )(normed, cotangent, up_weight, up_bias[None, :], down_weight)


def over_tensor(value):
    return lax.ppermute(value, "tensor", [(0, 1), (1, 0)])


def over_bit(value, bit, count):
    return lax.ppermute(value, "dp", [(i, i ^ (1 << bit)) for i in range(count)])


def other_half(weight, place, count):
    rows = weight.shape[0] // 4
    mine = place % 4
    piece = lax.dynamic_slice_in_dim(weight, mine * rows, rows, 0)
    first = over_tensor(piece)
    second = over_bit(first, 1, count)
    third = over_bit(jnp.stack([first, second]), 0, count)
    whole = jnp.zeros_like(weight)
    for offset, part in ((0, first), (2, second), (1, third[0]), (3, third[1])):
        whole = lax.dynamic_update_slice_in_dim(whole, part, (mine ^ offset) * rows, 0)
    return whole


def scatter_sum(grads, place, count):
    groups, width, columns = grads.shape
    bits = count.bit_length() - 1
    for bit in range(bits):
        left = count >> (bit + 1)
        split = grads.reshape(groups, left, 2, width // count, columns)
        mine = (place >> bit) & 1
        keep = lax.dynamic_index_in_dim(split, mine, 2, keepdims=False)
        send = lax.dynamic_index_in_dim(split, 1 - mine, 2, keepdims=False)
        got = over_bit(send, bit, count)
        grads = keep.astype(f32) + got.astype(f32)
        if bit < bits - 1:
            grads = grads.astype(bf16)
    return grads.reshape(groups, width // count, columns)


def all_sum(vector, count):
    for bit in range(count.bit_length() - 1):
        vector = vector + over_bit(vector, bit, count)
    return vector


def norm_parts(values):
    centre = values - jnp.mean(values, axis=-1, keepdims=True)
    spread = jnp.mean(centre * centre, axis=-1, keepdims=True)
    scale = lax.rsqrt(spread + EPS)
    return centre * scale, scale


def norm_back(grad, unit, scale, gain):
    c = grad * gain
    mean = jnp.mean(c, axis=-1, keepdims=True)
    along = jnp.mean(c * unit, axis=-1, keepdims=True)
    return scale * (c - mean - unit * along)


def on_device(
    count,
    patches,
    cotangent,
    clip_lengths,
    attn_gain,
    attn_shift,
    qkv_weight,
    qkv_bias,
    proj_weight,
    proj_bias,
    mlp_gain,
    mlp_shift,
    up_weight,
    up_bias,
    down_weight,
    down_bias,
):
    tokens, width = patches.shape
    half = tokens // 2
    local_width = proj_weight.shape[0]
    local_heads = local_width // HEAD_DIM
    side = lax.axis_index("tensor")
    place = lax.axis_index("dp")
    first_side = side == 0

    def pick(pair):
        mine = lax.dynamic_index_in_dim(pair, side, 0, keepdims=False)
        return mine, lax.dynamic_index_in_dim(pair, 1 - side, 0, keepdims=False)

    def my_rows(value):
        return lax.dynamic_slice_in_dim(value, side * half, half, 0)

    def both_rows(mine):
        theirs = over_tensor(mine)
        return jnp.concatenate(
            [jnp.where(first_side, mine, theirs), jnp.where(first_side, theirs, mine)], axis=0
        )

    proj_other = other_half(proj_weight, place, count)
    up_other = other_half(up_weight, place, count)
    down_other = other_half(down_weight, place, count)
    qkv_flat = qkv_weight.reshape(width, 3 * local_width)
    qkv_other = other_half(qkv_flat, place, count)

    clip_len = clip_lengths[0, 0]
    cosine, sine = rotary_angles(jnp.arange(tokens, dtype=jnp.int32) % clip_len)
    normed, qkv = qkv_forward(
        patches, attn_gain, attn_shift, qkv_flat, qkv_bias.reshape(-1), cosine, sine
    )

    heads_call = local_heads // FWD_CALLS
    weights, attended, totals, att_mine, att_other = [], [], [], [], []
    for call in range(FWD_CALLS):
        e, halves, whole, total = attend_forward(qkv, clip_lengths, call * heads_call, heads_call)
        keep, send = pick(halves)
        weights.append(e)
        attended.append(whole)
        totals.append(total)
        att_mine.append(keep)
        att_other.append(over_tensor(send))
    att_mine = jnp.concatenate(att_mine, axis=0)
    att_other = jnp.concatenate(att_other, axis=0)

    patch_rows = my_rows(patches).astype(f32)
    cot_rows = my_rows(cotangent)
    attn_out = dot(att_mine, proj_weight, 0, 0).astype(bf16).astype(f32) + dot(
        att_other, proj_other, 0, 0
    ).astype(bf16).astype(f32)
    residual = patch_rows + (attn_out + proj_bias)
    unit_two, scale_two = norm_parts(residual)
    normed_two = (unit_two * mlp_gain + mlp_shift).astype(bf16)

    up_bias_other = over_tensor(up_bias)
    out_a, ngrad_a, wgrad_a, bgrad_a = mlp(normed_two, cot_rows, up_weight, up_bias, down_weight)
    out_b, ngrad_b, wgrad_b, bgrad_b = mlp(
        normed_two, cot_rows, up_other, up_bias_other, down_other
    )
    mlp_out = out_a.astype(bf16).astype(f32) + out_b.astype(bf16).astype(f32)
    block_out = both_rows((residual + (mlp_out + down_bias)).astype(bf16))

    normed_two_grad = ngrad_a + ngrad_b
    mlp_gain_grad = jnp.sum(normed_two_grad * unit_two, axis=0)
    mlp_shift_grad = jnp.sum(normed_two_grad, axis=0)
    cot_wide = cot_rows.astype(f32)
    residual_grad = cot_wide + norm_back(normed_two_grad, unit_two, scale_two, mlp_gain)
    branch_low = residual_grad.astype(bf16)
    proj_bias_grad = jnp.sum(branch_low.astype(f32), axis=0)
    down_bias_grad = jnp.sum(cot_wide, axis=0)

    att_grad_send = dot(proj_other, branch_low, 1, 1).astype(bf16)
    att_grad_got = over_tensor(att_grad_send)
    att_grad_mine = dot(proj_weight, branch_low, 1, 1).astype(bf16)
    left = jnp.where(first_side, att_grad_mine, att_grad_got)
    right = jnp.where(first_side, att_grad_got, att_grad_mine)

    proj_grad = jnp.stack(
        [dot(branch_low, att_mine, 0, 1).astype(bf16), dot(branch_low, att_other, 0, 1).astype(bf16)]
    )

    heads_call = local_heads // BWD_CALLS
    mixed_whole, mixed_mine, mixed_other = [], [], []
    for call in range(BWD_CALLS):
        first = call * heads_call
        index, inner = divmod(first, local_heads // FWD_CALLS)
        halves, whole = attend_backward(
            weights[index],
            qkv,
            attended[index],
            totals[index],
            left,
            right,
            cosine,
            sine,
            first,
            inner,
            heads_call,
        )
        keep, send = pick(halves)
        mixed_whole.append(whole)
        mixed_mine.append(keep)
        mixed_other.append(over_tensor(send))
    mixed_whole = jnp.concatenate(mixed_whole, axis=1).reshape(3 * local_width, tokens)
    mixed_mine = jnp.concatenate(mixed_mine, axis=1).reshape(3 * local_width, half)
    mixed_other = jnp.concatenate(mixed_other, axis=1).reshape(3 * local_width, half)

    qkv_bias_grad = jnp.sum(mixed_whole.astype(f32), axis=1)
    normed_grad = dot(mixed_mine, qkv_flat, 0, 1) + dot(mixed_other, qkv_other, 0, 1)
    unit_one, scale_one = norm_parts(patch_rows)
    attn_gain_grad = jnp.sum(normed_grad * unit_one, axis=0)
    attn_shift_grad = jnp.sum(normed_grad, axis=0)
    patch_grad = both_rows(
        (residual_grad + norm_back(normed_grad, unit_one, scale_one, attn_gain)).astype(bf16)
    )

    qkv_grad = dot(normed, mixed_whole, 0, 1).astype(bf16)

    mlp_a = scatter_sum(wgrad_a, place, count)
    mlp_b = scatter_sum(wgrad_b, place, count)
    mlp_sum = mlp_a + over_tensor(mlp_b.astype(bf16)).astype(f32)
    proj_pair = scatter_sum(proj_grad, place, count)
    proj_sum = proj_pair[0] + over_tensor(proj_pair[1].astype(bf16)).astype(f32)
    qkv_sum = scatter_sum(qkv_grad[None], place, count)[0]

    early = jnp.concatenate([mlp_gain_grad, mlp_shift_grad, proj_bias_grad, down_bias_grad])
    got = over_tensor(jnp.concatenate([early, bgrad_b[0]]))
    early = all_sum(
        jnp.concatenate([early + got[: 4 * width], bgrad_a[0] + got[4 * width :]]), count
    )
    late = jnp.concatenate([attn_gain_grad, attn_shift_grad])
    late = late + over_tensor(late)
    late = all_sum(jnp.concatenate([late, qkv_bias_grad]), count)
    return (
        block_out,
        patch_grad,
        late[:width],
        late[width : 2 * width],
        qkv_sum.reshape(width // count, 3, local_width),
        late[2 * width :].reshape(3, local_width),
        proj_sum.T,
        early[2 * width : 3 * width],
        early[:width],
        early[width : 2 * width],
        mlp_sum[0],
        early[4 * width :],
        mlp_sum[1].T,
        early[3 * width : 4 * width],
    )


def solution(mesh):
    return jax.shard_map(
        functools.partial(on_device, mesh.shape["dp"]),
        mesh=mesh,
        in_specs=(
            P("dp", None),
            P("dp", None),
            P("dp", None),
            P(),
            P(),
            P(None, None, "tensor"),
            P(None, "tensor"),
            P("tensor", None),
            P(),
            P(),
            P(),
            P(None, "tensor"),
            P("tensor"),
            P("tensor", None),
            P(),
        ),
        out_specs=(
            P("dp", None),
            P("dp", None),
            P(),
            P(),
            P("dp", None, "tensor"),
            P(None, "tensor"),
            P("tensor", "dp"),
            P(),
            P(),
            P(),
            P("dp", "tensor"),
            P("tensor"),
            P("tensor", "dp"),
            P(),
        ),
        check_vma=False,
    )
```

time: 1360 us -> 730 us (0.54)
  waiting for transfers between devices: 842 us -> 233 us
  Pallas kernels: 0 us -> 182 us
  matrix products: 184 us -> 31.8 us
  starting transfers between devices: 0.46 us -> 109 us
  blocking collectives: 62.1 us -> 0 us
  loops' own time: 30.5 us -> 0 us
  other arithmetic: 88.4 us -> 61 us
  local copies, waits for them, and re-layouts: 125 us -> 106 us
  between operations: 17.2 us -> 2.38 us
    psum x3 -> x0, waiting for transfers between devices: 374 us -> none  [the longest x1 157 us: on_device(): lax.psum(down_part.astype(jnp.bfloat16), 'tensor').astype(jnp.float32)]
    unnamed x8 -> x0, waiting for transfers between devices: 269 us -> none
    ppermute x0 -> x52, waiting for transfers between devices: none -> 233 us  [the longest x32 163 us: over_bit(): return lax.ppermute(value, 'dp', [(i, i ^ 1 << bit) for i in range(count)])]
    reduce_scatter x3 -> x0, waiting for transfers between devices: 200 us -> none  [the longest x1 110 us: on_device(): lax.psum_scatter(up_weight_grad, 'dp', scatter_dimension=0, tiled=True)]
    pallas_call x0 -> x11, Pallas kernels: none -> 182 us  [the longest x2 65.1 us: mlp(): pl.pallas_call(mlp_kernel, grid=(hidden // FF_TILE,), out_shape=(jax.Shap...]
    dot_general x19 -> x9, matrix products: 184 us -> 31.8 us  [dot(): lax.dot_general(left, right, (((left_dim,), (right_dim,)), ((), ())), pre...]
    ppermute x0 -> x52, starting transfers between devices: none -> 109 us  [the longest x32 84 us: over_bit(): return lax.ppermute(value, 'dp', [(i, i ^ 1 << bit) for i in range(count)])]
    psum x1 -> x0, blocking collectives: 62.1 us -> none  [on_device(): lax.psum((attn_gain_grad, attn_shift_grad, qkv_bias_grad, proj_bias_grad,...]
  transfers between devices with their start and end apart: 7 -> 52, of which waited for: 6 -> 20; matrix products, arithmetic and copies ran while one was open for 7% -> 26% of each run, Pallas kernels for 0% -> 25%
where the time goes in v1:
time: 730 us; the launch traced here: 725 us
  waiting for transfers between devices  233 us (32%)
  Pallas kernels  182 us (25%)
  starting transfers between devices  109 us (15%)
  local copies, waits for them, and re-layouts  106 us (15%)
  other arithmetic  61 us (8%)
  matrix products  31.8 us (4%)
    ppermute x32, waiting for transfers between devices, over_bit(): return lax.ppermute(value, 'dp', [(i, i ^ 1 << bit) for i in range(count)])  163 us
    ppermute x32, starting transfers between devices, over_bit(): return lax.ppermute(value, 'dp', [(i, i ^ 1 << bit) for i in range(count)])  84 us
    ppermute x20, waiting for transfers between devices, over_tensor(): return lax.ppermute(value, 'tensor', [(0, 1), (1, 0)])  70.5 us
    pallas_call x2, Pallas kernels, mlp(): pl.pallas_call(mlp_kernel, grid=(hidden // FF_TILE,), out_shape=(jax.Shap...  65.1 us
    pallas_call x4, Pallas kernels, attend_backward(): pl.pallas_call(attend_back_kernel, grid=(heads,), out_shape=(jax.ShapeDty...  62.4 us
    pallas_call x4, Pallas kernels, attend_forward(): pl.pallas_call(attend_kernel, grid=(heads,), out_shape=(jax.ShapeDtypeStr...  39.5 us
    dot_general x9, matrix products, dot(): lax.dot_general(left, right, (((left_dim,), (right_dim,)), ((), ())), pre...  31.8 us
    ppermute x20, starting transfers between devices, over_tensor(): return lax.ppermute(value, 'tensor', [(0, 1), (1, 0)])  25 us
  transfers between devices with their start and end apart: 52, of which 20 were waited for; matrix products, arithmetic and copies ran while one was open for 26% of the time, Pallas kernels for 25%

profile of v1, /device:TPU:0, one launch (start us, length us, event | category | flops | bytes accessed | tf_op | source)
XLA Modules:
  0.0 724.7 jit_solution(1374813186767594493)
XLA Ops:
  0.7 3.0 collective-permute-start.10
  4.9 4.6 copy.118
  12.9 4.6 copy.119.w_ref
  20.4 14.8 %qkv_forward.1 = (bf16[1568,1024]{1,0:T(8,128)(2,1)}, bf16[1536,1568]{1,0:T(8,128)(2,1)}) custom-call(bf16[1568,1024]{1,0:T(8,128)(2,1)} %x_ref.1, f32[1,1024]{1,0:T(1,128)} %bitcast.260, f32[1,1024]{1,0:T(1,128)} %bitcast.265, bf16[1024,1536]{1,0:T(8,128)(2,1)} %copy.119.w_ref, f32[1536,1]{1,0:T(8,128)} %bitcast.247, ...), custom_call_target="tpu_custom_call" | custom-call | flops 4932501504 | bytes 14000000 | tf_op jit(solution)/shard_map/qkv_forward/pallas_call | solution.py:95
  35.2 9.8 %attend_forward.5 = (bf16[2,1568,1568]{2,1,0:T(8,128)(2,1)}, bf16[2,128,784]{2,1,0:T(8,128)(2,1)}, bf16[128,1568]{1,0:T(8,128)(2,1)}, f32[2,1,1568]{2,1,0:T(1,128)}) custom-call(s32[1,8]{1,0:T(1,128)} %len_ref.7, bf16[1536,1568]{1,0:T(8,128)(2,1)} %get-tuple-element.48.q_ref.k_ref.v_ref, bf16[1536,1568]{1,0:T(8,128)(2,1)} %get-tuple-element.48.q_ref.k_ref.v_ref, ...), custom_call_target="tpu_custom_call" | custom-call | flops 5035261952 | bytes 9834496 | tf_op jit(solution)/shard_map/attend_forward/pallas_call | solution.py:185
  48.0 10.0 %attend_forward.4 = (bf16[2,1568,1568]{2,1,0:T(8,128)(2,1)}, bf16[2,128,784]{2,1,0:T(8,128)(2,1)}, bf16[128,1568]{1,0:T(8,128)(2,1)}, f32[2,1,1568]{2,1,0:T(1,128)}) custom-call(s32[1,8]{1,0:T(1,128)} %len_ref.7, bf16[1536,1568]{1,0:T(8,128)(2,1)} %get-tuple-element.48.q_ref.k_ref.v_ref, bf16[1536,1568]{1,0:T(8,128)(2,1)} %get-tuple-element.48.q_ref.k_ref.v_ref, ...), custom_call_target="tpu_custom_call" | custom-call | flops 5035261952 | bytes 9834496 | tf_op jit(solution)/shard_map/attend_forward/pallas_call | solution.py:185
  60.8 9.7 %attend_forward.7 = (bf16[2,1568,1568]{2,1,0:T(8,128)(2,1)}, bf16[2,128,784]{2,1,0:T(8,128)(2,1)}, bf16[128,1568]{1,0:T(8,128)(2,1)}, f32[2,1,1568]{2,1,0:T(1,128)}) custom-call(s32[1,8]{1,0:T(1,128)} %len_ref.7, bf16[1536,1568]{1,0:T(8,128)(2,1)} %get-tuple-element.48.q_ref.k_ref.v_ref, bf16[1536,1568]{1,0:T(8,128)(2,1)} %get-tuple-element.48.q_ref.k_ref.v_ref, ...), custom_call_target="tpu_custom_call" | custom-call | flops 5035261952 | bytes 9834496 | tf_op jit(solution)/shard_map/attend_forward/pallas_call | solution.py:185
  70.4 10.0 %attend_forward.6 = (bf16[2,1568,1568]{2,1,0:T(8,128)(2,1)}, bf16[2,128,784]{2,1,0:T(8,128)(2,1)}, bf16[128,1568]{1,0:T(8,128)(2,1)}, f32[2,1,1568]{2,1,0:T(1,128)}) custom-call(s32[1,8]{1,0:T(1,128)} %len_ref.7, bf16[1536,1568]{1,0:T(8,128)(2,1)} %get-tuple-element.48.q_ref.k_ref.v_ref, bf16[1536,1568]{1,0:T(8,128)(2,1)} %get-tuple-element.48.q_ref.k_ref.v_ref, ...), custom_call_target="tpu_custom_call" | custom-call | flops 5035261952 | bytes 9834496 | tf_op jit(solution)/shard_map/attend_forward/pallas_call | solution.py:185
  84.9 2.3 constant_dynamic-slice_fusion.16
  89.4 2.2 convolution_convert_fusion.2
  93.2 2.3 constant_dynamic-slice_fusion.15
  96.6 35.3 %collective-permute-start.5 = (bf16[128,1024]{1,0:T(8,128)(2,1)S(1)}, bf16[128,1024]{1,0:T(8,128)(2,1)S(1)}, u32[]{:S(2)}, u32[]{:S(2)}) collective-permute-start(bf16[128,1024]{1,0:T(8,128)(2,1)S(1)} %collective-permute-done.4), channel_id=1, source_target_pairs={{0,4},{2,6},{4,0},{6,2},{8,12},{10,14},{12,8},{14,10},{16,20},{18,... | collective-permute-start | bytes 786440 | tf_op jit(solution)/shard_map/ppermute | solution.py:380
  138.1 12.3 %collective-permute-done.3 = bf16[128,784]{1,0:T(8,128)(2,1)S(1)} collective-permute-done((bf16[128,784]{1,0:T(8,128)(2,1)}, bf16[128,784]{1,0:T(8,128)(2,1)S(1)}, u32[]{:S(2)}, u32[]{:S(2)}) %collective-permute-start.3) | collective-permute-done | bytes 200736 | tf_op jit(solution)/shard_map/ppermute | solution.py:376
  152.1 2.2 broadcast_in_dim.110
  161.9 32.7 %feed_forward.2 = (f32[784,1024]{1,0:T(8,128)}, f32[784,1024]{1,0:T(8,128)}, bf16[2,1024,2048]{2,1,0:T(8,128)(2,1)}, f32[1,2048]{1,0:T(1,128)}) custom-call(bf16[784,1024]{1,0:T(8,128)(2,1)} %add_convert_fusion.1.n_ref, bf16[784,1024]{1,0:T(8,128)(2,1)} %get-tuple-element.175.c_ref, bf16[1024,2048]{1,0:T(8,128)(2,1)} %up_ref.1, f32[1,2048]{1,0:T(1,128)} %bitcast.263, ...), custom_call_target="tpu_custom_call" | custom-call | flops 19730006016 | bytes 24000000 | tf_op jit(solution)/shard_map/feed_forward/pallas_call | solution.py:343
  197.8 4.8 dynamic-slice_bitcast_fusion.1
  204.7 2.7 broadcast_in_dim.109
  208.4 2.5 broadcast_in_dim.107
  214.1 5.0 collective-permute-done.12
  219.4 2.4 constant_dynamic-update-slice_fusion.13
  229.7 32.4 %feed_forward.3 = (f32[784,1024]{1,0:T(8,128)}, f32[784,1024]{1,0:T(8,128)}, bf16[2,1024,2048]{2,1,0:T(8,128)(2,1)}, f32[1,2048]{1,0:T(1,128)}) custom-call(bf16[784,1024]{1,0:T(8,128)(2,1)} %add_convert_fusion.1.n_ref, bf16[784,1024]{1,0:T(8,128)(2,1)} %get-tuple-element.175.c_ref, bf16[1024,2048]{1,0:T(8,128)(2,1)} %fusion.35.up_ref, f32[1,2048]{1,0:T(1,128)} %bitcast.264, ...), custom_call_target="tpu_custom_call" | custom-call | flops 19730006016 | bytes 24000000 | tf_op jit(solution)/shard_map/feed_forward/pallas_call | solution.py:343
  262.2 5.6 multiply_reduce_fusion
  268.4 5.2 convert_reduce_fusion.3
  275.9 2.3 dynamic-slice_bitcast_fusion
  285.4 24.5 %collective-permute-start.41 = (f32[6144]{0:T(1024)S(1)}, f32[6144]{0:T(1024)S(1)}, u32[]{:S(2)}, u32[]{:S(2)}) collective-permute-start(f32[6144]{0:T(1024)S(1)} %add.397), channel_id=1, source_target_pairs={{0,8},{2,10},{4,12},{6,14},{8,0},{10,2},{12,4},{14,6},{16,24},{18,... | collective-permute-start | bytes 73736 | tf_op jit(solution)/shard_map/ppermute | solution.py:380
  311.8 2.7 collective-permute-start.42
  318.5 2.2 copy.122
  320.7 2.6 bitcast_select_fusion
  323.3 15.4 %attend_backward.7 = (bf16[2,3,128,784]{3,2,1,0:T(8,128)(2,1)}, bf16[3,128,1568]{2,1,0:T(8,128)(2,1)}) custom-call(bf16[2,1568,1568]{2,1,0:T(8,128)(2,1)} %get-tuple-element.69.e_ref, bf16[1536,1568]{1,0:T(8,128)(2,1)} %get-tuple-element.48.q_ref.k_ref.v_ref, bf16[1536,1568]{1,0:T(8,128)(2,1)} %get-tuple-element.48.q_ref.k_ref.v_ref, ...), custom_call_target="tpu_custom_call" | custom-call | flops 10070523904 | bytes 9834496 | tf_op jit(solution)/shard_map/attend_backward/pallas_call | solution.py:267
  338.7 2.3 constant_dynamic-slice_fusion.7
  341.0 2.2 copy.131
  343.2 15.9 %attend_backward.6 = (bf16[2,3,128,784]{3,2,1,0:T(8,128)(2,1)}, bf16[3,128,1568]{2,1,0:T(8,128)(2,1)}) custom-call(bf16[2,1568,1568]{2,1,0:T(8,128)(2,1)} %get-tuple-element.65.e_ref, bf16[1536,1568]{1,0:T(8,128)(2,1)} %get-tuple-element.48.q_ref.k_ref.v_ref, bf16[1536,1568]{1,0:T(8,128)(2,1)} %get-tuple-element.48.q_ref.k_ref.v_ref, ...), custom_call_target="tpu_custom_call" | custom-call | flops 10070523904 | bytes 9834496 | tf_op jit(solution)/shard_map/attend_backward/pallas_call | solution.py:267
  359.1 2.6 constant_dynamic-slice_fusion.8
  361.6 2.2 copy.130
  363.8 15.4 %attend_backward.5 = (bf16[2,3,128,784]{3,2,1,0:T(8,128)(2,1)}, bf16[3,128,1568]{2,1,0:T(8,128)(2,1)}) custom-call(bf16[2,1568,1568]{2,1,0:T(8,128)(2,1)} %get-tuple-element.61.e_ref, bf16[1536,1568]{1,0:T(8,128)(2,1)} %get-tuple-element.48.q_ref.k_ref.v_ref, bf16[1536,1568]{1,0:T(8,128)(2,1)} %get-tuple-element.48.q_ref.k_ref.v_ref, ...), custom_call_target="tpu_custom_call" | custom-call | flops 10070523904 | bytes 9834496 | tf_op jit(solution)/shard_map/attend_backward/pallas_call | solution.py:267
  379.2 2.5 constant_dynamic-slice_fusion.9
  381.7 15.6 %attend_backward.4 = (bf16[2,3,128,784]{3,2,1,0:T(8,128)(2,1)}, bf16[3,128,1568]{2,1,0:T(8,128)(2,1)}) custom-call(bf16[2,1568,1568]{2,1,0:T(8,128)(2,1)} %get-tuple-element.57.e_ref, bf16[1536,1568]{1,0:T(8,128)(2,1)} %get-tuple-element.48.q_ref.k_ref.v_ref, bf16[1536,1568]{1,0:T(8,128)(2,1)} %get-tuple-element.48.q_ref.k_ref.v_ref, ...), custom_call_target="tpu_custom_call" | custom-call | flops 10070523904 | bytes 9834496 | tf_op jit(solution)/shard_map/attend_backward/pallas_call | solution.py:267
  397.4 2.5 constant_dynamic-slice_fusion.10
  399.8 2.2 copy.128
  404.2 2.2 copy.125
  406.3 2.2 copy.124
  408.5 2.2 copy.126
  416.9 2.3 copy-done.7
  420.0 7.0 fusion.17
  427.0 6.5 convolution_convert_fusion
  438.3 3.0 collective-permute-done.16
  442.5 11.8 %collective-permute-done.18 = bf16[3,128,784]{1,2,0:T(8,128)(2,1)} collective-permute-done((bf16[3,128,784]{1,2,0:T(8,128)(2,1)}, bf16[3,128,784]{1,2,0:T(8,128)(2,1)}, u32[]{:S(2)}, u32[]{:S(2)}) %collective-permute-start.18) | collective-permute-done | bytes 602144 | tf_op jit(solution)/shard_map/ppermute | solution.py:376
  454.2 12.8 %collective-permute-done.19 = bf16[3,128,784]{1,2,0:T(8,128)(2,1)S(1)} collective-permute-done((bf16[3,128,784]{1,2,0:T(8,128)(2,1)S(1)}, bf16[3,128,784]{1,2,0:T(8,128)(2,1)S(1)}, u32[]{:S(2)}, u32[]{:S(2)}) %collective-permute-start.19) | collective-permute-done | bytes 602144 | tf_op jit(solution)/shard_map/ppermute | solution.py:376
  469.9 2.9 copy.132
  472.8 8.2 %fusion.14 = (f32[1024]{0:T(1024)S(1)}, f32[784]{0:T(1024)S(1)}, f32[784]{0:T(1024)S(1)}, f32[1024]{0:T(1024)S(1)}, f32[784,1024]{1,0:T(8,128)S(1)}) fusion(f32[784]{0:T(1024)S(1)} %copy-done.39, f32[784]{0:T(1024)S(1)} %copy-done.38, bf16[1568,1024]{1,0:T(8,128)(2,1)} %x_ref.1, s32[]{:T(128)S(6)} %select_n.259, f32[1024]{0:T(1024)S(1)} %copy-done.45, ...), kind=kOutput, calls=%fused_computation.27 | convolution fusion | flops 2475078144 | bytes 13607172 | tf_op jit(solution)/shard_map/dot_general | solution.py:29
  481.8 5.4 fusion.1
  487.2 13.9 %collective-permute-done.24 = f32[2048]{0:T(1024)S(1)} collective-permute-done((f32[2048]{0:T(1024)S(1)}, f32[2048]{0:T(1024)S(1)}, u32[]{:S(2)}, u32[]{:S(2)}) %collective-permute-start.24) | collective-permute-done | bytes 8224 | tf_op jit(solution)/shard_map/ppermute | solution.py:376
  503.3 3.3 collective-permute-done.26
  506.6 6.9 collective-permute-start.27
  528.6 3.3 collective-permute-done.36
  533.9 5.4 fusion
  545.6 14.5 %collective-permute-done.37 = bf16[64,512]{1,0:T(8,128)(2,1)S(1)} collective-permute-done((bf16[64,512]{1,0:T(8,128)(2,1)S(1)}, bf16[64,512]{1,0:T(8,128)(2,1)S(1)}, u32[]{:S(2)}, u32[]{:S(2)}) %collective-permute-start.37) | collective-permute-done | bytes 65568 | tf_op jit(solution)/shard_map/ppermute | solution.py:376
  561.0 67.5 %collective-permute-done.30 = bf16[1,4,64,1536]{3,2,1,0:T(8,128)(2,1)S(1)} collective-permute-done((bf16[1,4,64,1536]{3,2,1,0:T(8,128)(2,1)S(1)}, bf16[1,4,64,1536]{3,2,1,0:T(8,128)(2,1)S(1)}, u32[]{:S(2)}, u32[]{:S(2)}) %collective-permute-start.30) | collective-permute-done | bytes 786464 | tf_op jit(solution)/shard_map/ppermute | solution.py:380
  632.2 2.4 fusion.3
  636.4 6.6 collective-permute-done.31
  643.2 30.0 %collective-permute-done.49 = bf16[2,2,64,2048]{3,2,0,1:T(8,128)(2,1)S(1)} collective-permute-done((bf16[2,2,64,2048]{3,2,0,1:T(8,128)(2,1)S(1)}, bf16[2,2,64,2048]{3,2,0,1:T(8,128)(2,1)S(1)}, u32[]{:S(2)}, u32[]{:S(2)}) %collective-permute-start.49) | collective-permute-done | bytes 1048608 | tf_op jit(solution)/shard_map/ppermute | solution.py:380
  673.7 22.2 %collective-permute-done.45 = bf16[2,2,64,2048]{3,2,1,0:T(8,128)(2,1)S(1)} collective-permute-done((bf16[2,2,64,2048]{3,2,1,0:T(8,128)(2,1)S(1)}, bf16[2,2,64,2048]{3,2,1,0:T(8,128)(2,1)S(1)}, u32[]{:S(2)}, u32[]{:S(2)}) %collective-permute-start.45) | collective-permute-done | bytes 1048608 | tf_op jit(solution)/shard_map/ppermute | solution.py:380
  697.2 14.3 %collective-permute-done.50 = bf16[2,1,64,2048]{3,2,0,1:T(8,128)(2,1)S(1)} collective-permute-done((bf16[2,1,64,2048]{3,2,0,1:T(8,128)(2,1)S(1)}, bf16[2,1,64,2048]{3,2,0,1:T(8,128)(2,1)S(1)}, u32[]{:S(2)}, u32[]{:S(2)}) %collective-permute-start.50) | collective-permute-done | bytes 524320 | tf_op jit(solution)/shard_map/ppermute | solution.py:380
  716.8 5.1 collective-permute-done.46
  (317 shorter events, 131.4 us)
Async XLA Ops:
  0.7 228.5 %collective-permute-start.10 = (f32[2048]{0:T(1024)}, f32[2048]{0:T(1024)S(1)}, u32[]{:S(2)}, u32[]{:S(2)}) collective-permute-start(f32[2048]{0:T(1024)} %param.27), channel_id=1, source_target_pairs={{0,1},{1,0},{2,3},{3,2},{4,5},{5,4},{6,7},{7,6},{8,9},{9,8},{10,11... | collective-permute-start | bytes 24584 | tf_op jit(solution)/shard_map/ppermute | solution.py:376
  3.7 92.9 %collective-permute-start.4 = (bf16[128,1024]{1,0:T(8,128)(2,1)S(1)}, bf16[128,1024]{1,0:T(8,128)(2,1)S(1)}, u32[]{:S(2)}, u32[]{:S(2)}) collective-permute-start(bf16[128,1024]{1,0:T(8,128)(2,1)S(1)} %constant_dynamic-slice_fusion.18), channel_id=1, source_target_pairs={{0,1},{1,0},{2,3},{3,2},{4,5},{5,4},{6,7},{7,6},{8,9},{9,8},{10,11... | collective-permute-start | bytes 786440 | tf_op jit(solution)/shard_map/ppermute | solution.py:376
  4.9 7.6 %copy-start.46 = (s32[1,8]{1,0:T(1,128)S(1)}, s32[1,8]{1,0:T(1,128)}, u32[]{:S(2)}) copy-start(s32[1,8]{1,0:T(1,128)} %len_ref.7) | copy-start | bytes 100
  11.6 140.2 %collective-permute-start.20 = (bf16[256,1536]{0,1:T(8,128)(2,1)}, bf16[256,1536]{0,1:T(8,128)(2,1)S(1)}, u32[]{:S(2)}, u32[]{:S(2)}) collective-permute-start(bf16[256,1536]{0,1:T(8,128)(2,1)} %constant_dynamic-slice_fusion.6), channel_id=1, source_target_pairs={{0,1},{1,0},{2,3},{3,2},{4,5},{5,4},{6,7},{7,6},{8,9},{9,8},{10,11... | collective-permute-start | bytes 2359304 | tf_op jit(solution)/shard_map/ppermute | solution.py:376
  46.9 86.0 %collective-permute-start.1 = (bf16[128,784]{1,0:T(8,128)(2,1)}, bf16[128,784]{1,0:T(8,128)(2,1)}, u32[]{:S(2)}, u32[]{:S(2)}) collective-permute-start(bf16[128,784]{1,0:T(8,128)(2,1)} %get-tuple-element.203), channel_id=1, source_target_pairs={{0,1},{1,0},{2,3},{3,2},{4,5},{5,4},{6,7},{7,6},{8,9},{9,8},{10,11... | collective-permute-start | bytes 602120 | tf_op jit(solution)/shard_map/ppermute | solution.py:376
  59.9 35.6 %collective-permute-start = (bf16[128,784]{1,0:T(8,128)(2,1)}, bf16[128,784]{1,0:T(8,128)(2,1)}, u32[]{:S(2)}, u32[]{:S(2)}) collective-permute-start(bf16[128,784]{1,0:T(8,128)(2,1)} %get-tuple-element.205), channel_id=1, source_target_pairs={{0,1},{1,0},{2,3},{3,2},{4,5},{5,4},{6,7},{7,6},{8,9},{9,8},{10,11... | collective-permute-start | bytes 602120 | tf_op jit(solution)/shard_map/ppermute | solution.py:376
  80.4 7.5 %copy-start.25 = (bf16[2,128,784]{2,1,0:T(8,128)(2,1)S(1)}, bf16[2,128,784]{2,1,0:T(8,128)(2,1)}, u32[]{:S(2)}) copy-start(bf16[2,128,784]{2,1,0:T(8,128)(2,1)} %get-tuple-element.51) | copy-start | bytes 1204228
  80.4 9.0 %copy-start.26 = (bf16[128,784]{1,0:T(8,128)(2,1)S(1)}, bf16[128,784]{1,0:T(8,128)(2,1)}, u32[]{:S(2)}) copy-start(bf16[128,784]{1,0:T(8,128)(2,1)} %get-tuple-element.204) | copy-start | bytes 602116
  80.4 9.0 %copy-start.28 = (bf16[128,784]{1,0:T(8,128)(2,1)S(1)}, bf16[128,784]{1,0:T(8,128)(2,1)}, u32[]{:S(2)}) copy-start(bf16[128,784]{1,0:T(8,128)(2,1)} %get-tuple-element.206) | copy-start | bytes 602116
  82.3 9.3 %copy-start.37 = (f32[784]{0:T(1024)}, f32[784]{0:T(1024)S(1)}, u32[]{:S(2)}) copy-start(f32[784]{0:T(1024)S(1)} %broadcast_multiply_fusion.2) | copy-start | bytes 9412
  95.4 39.3 %collective-permute-start.2 = (bf16[128,784]{1,0:T(8,128)(2,1)}, bf16[128,784]{1,0:T(8,128)(2,1)S(1)}, u32[]{:S(2)}, u32[]{:S(2)}) collective-permute-start(bf16[128,784]{1,0:T(8,128)(2,1)} %get-tuple-element.201), channel_id=1, source_target_pairs={{0,1},{1,0},{2,3},{3,2},{4,5},{5,4},{6,7},{7,6},{8,9},{9,8},{10,11... | collective-permute-start | bytes 602120 | tf_op jit(solution)/shard_map/ppermute | solution.py:376
  96.6 39.4 %copy-start.20 = (bf16[128,1024]{1,0:T(8,128)(2,1)}, bf16[128,1024]{1,0:T(8,128)(2,1)S(1)}, u32[]{:S(2)}) copy-start(bf16[128,1024]{1,0:T(8,128)(2,1)S(1)} %collective-permute-done.4) | copy-start | bytes 786436
  96.6 39.6 %collective-permute-start.5 = (bf16[128,1024]{1,0:T(8,128)(2,1)S(1)}, bf16[128,1024]{1,0:T(8,128)(2,1)S(1)}, u32[]{:S(2)}, u32[]{:S(2)}) collective-permute-start(bf16[128,1024]{1,0:T(8,128)(2,1)S(1)} %collective-permute-done.4), channel_id=1, source_target_pairs={{0,4},{2,6},{4,0},{6,2},{8,12},{10,14},{12,8},{14,10},{16,20},{18,... | collective-permute-start | bytes 786440 | tf_op jit(solution)/shard_map/ppermute | solution.py:380
  132.9 61.8 %collective-permute-start.11 = (bf16[512,1024]{1,0:T(8,128)(2,1)}, bf16[512,1024]{1,0:T(8,128)(2,1)S(1)}, u32[]{:S(2)}, u32[]{:S(2)}) collective-permute-start(bf16[512,1024]{1,0:T(8,128)(2,1)} %constant_dynamic-slice_fusion.15), channel_id=1, source_target_pairs={{0,1},{1,0},{2,3},{3,2},{4,5},{5,4},{6,7},{7,6},{8,9},{9,8},{10,11... | collective-permute-start | bytes 3145736 | tf_op jit(solution)/shard_map/ppermute | solution.py:376
  134.8 15.6 %collective-permute-start.3 = (bf16[128,784]{1,0:T(8,128)(2,1)}, bf16[128,784]{1,0:T(8,128)(2,1)S(1)}, u32[]{:S(2)}, u32[]{:S(2)}) collective-permute-start(bf16[128,784]{1,0:T(8,128)(2,1)} %get-tuple-element.199), channel_id=1, source_target_pairs={{0,1},{1,0},{2,3},{3,2},{4,5},{5,4},{6,7},{7,6},{8,9},{9,8},{10,11... | collective-permute-start | bytes 602120 | tf_op jit(solution)/shard_map/ppermute | solution.py:376
  136.2 25.4 %collective-permute-start.7 = (bf16[256,2048]{1,0:T(8,128)(2,1)}, bf16[256,2048]{1,0:T(8,128)(2,1)S(1)}, u32[]{:S(2)}, u32[]{:S(2)}) collective-permute-start(bf16[256,2048]{1,0:T(8,128)(2,1)} %constant_dynamic-slice_fusion.16), channel_id=1, source_target_pairs={{0,1},{1,0},{2,3},{3,2},{4,5},{5,4},{6,7},{7,6},{8,9},{9,8},{10,11... | collective-permute-start | bytes 3145736 | tf_op jit(solution)/shard_map/ppermute | solution.py:376
  150.4 5.0 collective-permute-start.6
  151.8 44.6 %collective-permute-start.21 = (bf16[256,1536]{0,1:T(8,128)(2,1)S(1)}, bf16[256,1536]{0,1:T(8,128)(2,1)}, u32[]{:S(2)}, u32[]{:S(2)}) collective-permute-start(bf16[256,1536]{0,1:T(8,128)(2,1)S(1)} %collective-permute-done.20), channel_id=1, source_target_pairs={{0,4},{2,6},{4,0},{6,2},{8,12},{10,14},{12,8},{14,10},{16,20},{18,... | collective-permute-start | bytes 2359304 | tf_op jit(solution)/shard_map/ppermute | solution.py:380
  161.6 41.5 %collective-permute-start.8 = (bf16[256,2048]{1,0:T(8,128)(2,1)S(1)}, bf16[256,2048]{1,0:T(8,128)(2,1)}, u32[]{:S(2)}, u32[]{:S(2)}) collective-permute-start(bf16[256,2048]{1,0:T(8,128)(2,1)S(1)} %collective-permute-done.7), channel_id=1, source_target_pairs={{0,4},{2,6},{4,0},{6,2},{8,12},{10,14},{12,8},{14,10},{16,20},{18,... | collective-permute-start | bytes 3145736 | tf_op jit(solution)/shard_map/ppermute | solution.py:380
  194.6 24.5 %collective-permute-start.12 = (bf16[512,1024]{1,0:T(8,128)(2,1)S(1)}, bf16[512,1024]{1,0:T(8,128)(2,1)S(1)}, u32[]{:S(2)}, u32[]{:S(2)}) collective-permute-start(bf16[512,1024]{1,0:T(8,128)(2,1)S(1)} %collective-permute-done.11), channel_id=1, source_target_pairs={{0,4},{2,6},{4,0},{6,2},{8,12},{10,14},{12,8},{14,10},{16,20},{18,... | collective-permute-start | bytes 3145736 | tf_op jit(solution)/shard_map/ppermute | solution.py:380
  197.7 25.2 %collective-permute-start.22 = (bf16[2,256,1536]{1,2,0:T(8,128)(2,1)S(1)}, bf16[2,256,1536]{1,2,0:T(8,128)(2,1)S(1)}, u32[]{:S(2)}, u32[]{:S(2)}) collective-permute-start(bf16[2,256,1536]{1,2,0:T(8,128)(2,1)S(1)} %pad_maximum_fusion.5), channel_id=1, source_target_pairs={{0,2},{2,0},{4,6},{6,4},{8,10},{10,8},{12,14},{14,12},{16,18},{18,... | collective-permute-start | bytes 4718600 | tf_op jit(solution)/shard_map/ppermute | solution.py:380
  202.7 278.4 %collective-permute-start.43 = (bf16[2,8,64,2048]{3,2,1,0:T(8,128)(2,1)}, bf16[2,8,64,2048]{3,2,1,0:T(8,128)(2,1)}, u32[]{:S(2)}, u32[]{:S(2)}) collective-permute-start(bf16[2,8,64,2048]{3,2,1,0:T(8,128)(2,1)} %dynamic-slice_bitcast_fusion.1), channel_id=1, source_target_pairs={{0,2},{2,0},{4,6},{6,4},{8,10},{10,8},{12,14},{14,12},{16,18},{18,... | collective-permute-start | bytes 12582920 | tf_op jit(solution)/shard_map/ppermute | solution.py:380
  204.6 20.3 %collective-permute-start.9 = (bf16[2,256,2048]{2,1,0:T(8,128)(2,1)S(1)}, bf16[2,256,2048]{2,1,0:T(8,128)(2,1)S(1)}, u32[]{:S(2)}, u32[]{:S(2)}) collective-permute-start(bf16[2,256,2048]{2,1,0:T(8,128)(2,1)S(1)} %pad_maximum_fusion.3), channel_id=1, source_target_pairs={{0,2},{2,0},{4,6},{6,4},{8,10},{10,8},{12,14},{14,12},{16,18},{18,... | collective-permute-start | bytes 6291464 | tf_op jit(solution)/shard_map/ppermute | solution.py:380
  219.3 7.7 %collective-permute-start.13 = (bf16[2,512,1024]{2,1,0:T(8,128)(2,1)S(1)}, bf16[2,512,1024]{2,1,0:T(8,128)(2,1)S(1)}, u32[]{:S(2)}, u32[]{:S(2)}) collective-permute-start(bf16[2,512,1024]{2,1,0:T(8,128)(2,1)S(1)} %pad_maximum_fusion.4), channel_id=1, source_target_pairs={{0,2},{2,0},{4,6},{6,4},{8,10},{10,8},{12,14},{14,12},{16,18},{18,... | collective-permute-start | bytes 6291464 | tf_op jit(solution)/shard_map/ppermute | solution.py:380
  262.2 13.7 %slice-start = ((s8[8388608]{0:T(1024)(128)(4,1)}), s8[4194304]{0:T(1024)(128)(4,1)S(1)}, s32[]{:S(2)}) async-start(s8[8388608]{0:T(1024)(128)(4,1)} %bitcast.219), calls=%async_computation | async-start | bytes 8388608
  268.4 7.5 %slice-start.1 = ((s8[8388608]{0:T(1024)(128)(4,1)}), s8[4194304]{0:T(1024)(128)(4,1)S(1)}, s32[]{:S(2)}) async-start(s8[8388608]{0:T(1024)(128)(4,1)} %bitcast.219), calls=%async_computation.1 | async-start | bytes 8388608
  273.6 4.6 collective-permute-start.38
  278.3 3.2 collective-permute-start.39
  280.3 38.2 %collective-permute-start.15 = (bf16[512,784]{0,1:T(8,128)(2,1)}, bf16[512,784]{0,1:T(8,128)(2,1)}, u32[]{:S(2)}, u32[]{:S(2)}) collective-permute-start(bf16[512,784]{0,1:T(8,128)(2,1)} %convolution_convert_fusion.5), channel_id=1, source_target_pairs={{0,1},{1,0},{2,3},{3,2},{4,5},{5,4},{6,7},{7,6},{8,9},{9,8},{10,11... | collective-permute-start | bytes 2408456 | tf_op jit(solution)/shard_map/ppermute | solution.py:376
  281.5 3.9 collective-permute-start.40
  285.4 26.4 %collective-permute-start.41 = (f32[6144]{0:T(1024)S(1)}, f32[6144]{0:T(1024)S(1)}, u32[]{:S(2)}, u32[]{:S(2)}) collective-permute-start(f32[6144]{0:T(1024)S(1)} %add.397), channel_id=1, source_target_pairs={{0,8},{2,10},{4,12},{6,14},{8,0},{10,2},{12,4},{14,6},{16,24},{18,... | collective-permute-start | bytes 73736 | tf_op jit(solution)/shard_map/ppermute | solution.py:380
  311.8 5.4 collective-permute-start.42
  317.2 116.3 %collective-permute-start.33 = (bf16[2,8,64,512]{3,2,1,0:T(8,128)(2,1)}, bf16[2,8,64,512]{3,2,1,0:T(8,128)(2,1)}, u32[]{:S(2)}, u32[]{:S(2)}) collective-permute-start(bf16[2,8,64,512]{3,2,1,0:T(8,128)(2,1)} %fusion.30), channel_id=1, source_target_pairs={{0,2},{2,0},{4,6},{6,4},{8,10},{10,8},{12,14},{14,12},{16,18},{18,... | collective-permute-start | bytes 3145736 | tf_op jit(solution)/shard_map/ppermute | solution.py:380
  411.7 26.6 %collective-permute-start.17 = (bf16[3,128,784]{1,2,0:T(8,128)(2,1)}, bf16[3,128,784]{1,2,0:T(8,128)(2,1)}, u32[]{:S(2)}, u32[]{:S(2)}) collective-permute-start(bf16[3,128,784]{1,2,0:T(8,128)(2,1)} %bitcast.251), channel_id=1, source_target_pairs={{0,1},{1,0},{2,3},{3,2},{4,5},{5,4},{6,7},{7,6},{8,9},{9,8},{10,11... | collective-permute-start | bytes 1806344 | tf_op jit(solution)/shard_map/ppermute | solution.py:376
  412.7 28.6 %collective-permute-start.16 = (bf16[3,128,784]{1,2,0:T(8,128)(2,1)}, bf16[3,128,784]{1,2,0:T(8,128)(2,1)}, u32[]{:S(2)}, u32[]{:S(2)}) collective-permute-start(bf16[3,128,784]{1,2,0:T(8,128)(2,1)} %bitcast.250), channel_id=1, source_target_pairs={{0,1},{1,0},{2,3},{3,2},{4,5},{5,4},{6,7},{7,6},{8,9},{9,8},{10,11... | collective-permute-start | bytes 1806344 | tf_op jit(solution)/shard_map/ppermute | solution.py:376
  413.7 40.5 %collective-permute-start.18 = (bf16[3,128,784]{1,2,0:T(8,128)(2,1)}, bf16[3,128,784]{1,2,0:T(8,128)(2,1)}, u32[]{:S(2)}, u32[]{:S(2)}) collective-permute-start(bf16[3,128,784]{1,2,0:T(8,128)(2,1)} %bitcast.249), channel_id=1, source_target_pairs={{0,1},{1,0},{2,3},{3,2},{4,5},{5,4},{6,7},{7,6},{8,9},{9,8},{10,11... | collective-permute-start | bytes 1806344 | tf_op jit(solution)/shard_map/ppermute | solution.py:376
  433.5 33.5 %collective-permute-start.19 = (bf16[3,128,784]{1,2,0:T(8,128)(2,1)S(1)}, bf16[3,128,784]{1,2,0:T(8,128)(2,1)S(1)}, u32[]{:S(2)}, u32[]{:S(2)}) collective-permute-start(bf16[3,128,784]{1,2,0:T(8,128)(2,1)S(1)} %bitcast.248), channel_id=1, source_target_pairs={{0,1},{1,0},{2,3},{3,2},{4,5},{5,4},{6,7},{7,6},{8,9},{9,8},{10,11... | collective-permute-start | bytes 1806344 | tf_op jit(solution)/shard_map/ppermute | solution.py:376
  438.3 95.6 %collective-permute-start.47 = (bf16[2,8,64,2048]{3,2,1,0:T(8,128)(2,1)}, bf16[2,8,64,2048]{3,2,1,0:T(8,128)(2,1)}, u32[]{:S(2)}, u32[]{:S(2)}) collective-permute-start(bf16[2,8,64,2048]{3,2,1,0:T(8,128)(2,1)} %dynamic-slice_bitcast_fusion), channel_id=1, source_target_pairs={{0,2},{2,0},{4,6},{6,4},{8,10},{10,8},{12,14},{14,12},{16,18},{18,... | collective-permute-start | bytes 12582920 | tf_op jit(solution)/shard_map/ppermute | solution.py:380
  441.3 84.6 %collective-permute-start.14 = (bf16[784,1024]{1,0:T(8,128)(2,1)}, bf16[784,1024]{1,0:T(8,128)(2,1)}, u32[]{:S(2)}, u32[]{:S(2)}) collective-permute-start(bf16[784,1024]{1,0:T(8,128)(2,1)} %get-tuple-element.182), channel_id=1, source_target_pairs={{0,1},{1,0},{2,3},{3,2},{4,5},{5,4},{6,7},{7,6},{8,9},{9,8},{10,11... | collective-permute-start | bytes 4816904 | tf_op jit(solution)/shard_map/ppermute | solution.py:376
  454.2 85.7 %collective-permute-start.29 = (bf16[1,8,64,1536]{3,2,1,0:T(8,128)(2,1)}, bf16[1,8,64,1536]{3,2,1,0:T(8,128)(2,1)}, u32[]{:S(2)}, u32[]{:S(2)}) collective-permute-start(bf16[1,8,64,1536]{3,2,1,0:T(8,128)(2,1)} %dynamic-slice_bitcast_fusion.4), channel_id=1, source_target_pairs={{0,2},{2,0},{4,6},{6,4},{8,10},{10,8},{12,14},{14,12},{16,18},{18,... | collective-permute-start | bytes 4718600 | tf_op jit(solution)/shard_map/ppermute | solution.py:380
  467.0 49.4 %collective-permute-start.34 = (bf16[2,4,64,512]{3,2,1,0:T(8,128)(2,1)}, bf16[2,4,64,512]{3,2,1,0:T(8,128)(2,1)}, u32[]{:S(2)}, u32[]{:S(2)}) collective-permute-start(bf16[2,4,64,512]{3,2,1,0:T(8,128)(2,1)} %dynamic-slice_bitcast_fusion.7), channel_id=1, source_target_pairs={{0,4},{2,6},{4,0},{6,2},{8,12},{10,14},{12,8},{14,10},{16,20},{18,... | collective-permute-start | bytes 1572872 | tf_op jit(solution)/shard_map/ppermute | solution.py:380
  481.0 20.2 %collective-permute-start.24 = (f32[2048]{0:T(1024)S(1)}, f32[2048]{0:T(1024)S(1)}, u32[]{:S(2)}, u32[]{:S(2)}) collective-permute-start(f32[2048]{0:T(1024)S(1)} %pad_maximum_fusion.12), channel_id=1, source_target_pairs={{0,1},{1,0},{2,3},{3,2},{4,5},{5,4},{6,7},{7,6},{8,9},{9,8},{10,11... | collective-permute-start | bytes 24584 | tf_op jit(solution)/shard_map/ppermute | solution.py:376
  487.2 30.4 %copy-start.4 = (bf16[2,8,64,2048]{3,2,1,0:T(8,128)(2,1)}, bf16[2,8,64,2048]{3,2,1,0:T(8,128)(2,1)S(1)}, u32[]{:S(2)}) copy-start(bf16[2,8,64,2048]{3,2,1,0:T(8,128)(2,1)S(1)} %fusion.1) | copy-start | bytes 12582916
  501.2 1.6 collective-permute-start.25
  501.3 18.5 %copy-start.6 = (f32[784,1024]{1,0:T(8,128)S(1)}, f32[784,1024]{1,0:T(8,128)}, u32[]{:S(2)}) copy-start(f32[784,1024]{1,0:T(8,128)} %get-tuple-element.178) | copy-start | bytes 9633796
  501.3 18.5 %copy-start.10 = (bf16[1568,1024]{1,0:T(8,128)(2,1)S(1)}, bf16[1568,1024]{1,0:T(8,128)(2,1)}, u32[]{:S(2)}) copy-start(bf16[1568,1024]{1,0:T(8,128)(2,1)} %x_ref.1) | copy-start | bytes 9633796
  502.8 3.8 collective-permute-start.26
  506.6 8.6 %collective-permute-start.27 = (f32[3584]{0:T(1024)S(1)}, f32[3584]{0:T(1024)S(1)}, u32[]{:S(2)}, u32[]{:S(2)}) collective-permute-start(f32[3584]{0:T(1024)S(1)} %add.374), channel_id=1, source_target_pairs={{0,8},{2,10},{4,12},{6,14},{8,0},{10,2},{12,4},{14,6},{16,24},{18,... | collective-permute-start | bytes 43016 | tf_op jit(solution)/shard_map/ppermute | solution.py:380
  515.2 6.1 collective-permute-start.28
  517.7 6.6 collective-permute-start.35
  521.3 110.7 %collective-permute-start.44 = (bf16[2,4,64,2048]{3,2,1,0:T(8,128)(2,1)}, bf16[2,4,64,2048]{3,2,1,0:T(8,128)(2,1)}, u32[]{:S(2)}, u32[]{:S(2)}) collective-permute-start(bf16[2,4,64,2048]{3,2,1,0:T(8,128)(2,1)} %dynamic-slice_bitcast_fusion.3), channel_id=1, source_target_pairs={{0,4},{2,6},{4,0},{6,2},{8,12},{10,14},{12,8},{14,10},{16,20},{18,... | collective-permute-start | bytes 6291464 | tf_op jit(solution)/shard_map/ppermute | solution.py:380
  524.3 36.5 %collective-permute-start.23 = (bf16[784,1024]{1,0:T(8,128)(2,1)S(1)}, bf16[784,1024]{1,0:T(8,128)(2,1)S(1)}, u32[]{:S(2)}, u32[]{:S(2)}) collective-permute-start(bf16[784,1024]{1,0:T(8,128)(2,1)S(1)} %fusion.13), channel_id=1, source_target_pairs={{0,1},{1,0},{2,3},{3,2},{4,5},{5,4},{6,7},{7,6},{8,9},{9,8},{10,11... | collective-permute-start | bytes 4816904 | tf_op jit(solution)/shard_map/ppermute | solution.py:376
  526.0 5.9 collective-permute-start.36
  532.0 28.2 %collective-permute-start.37 = (bf16[64,512]{1,0:T(8,128)(2,1)S(1)}, bf16[64,512]{1,0:T(8,128)(2,1)S(1)}, u32[]{:S(2)}, u32[]{:S(2)}) collective-permute-start(bf16[64,512]{1,0:T(8,128)(2,1)S(1)} %fusion.49), channel_id=1, source_target_pairs={{0,1},{1,0},{2,3},{3,2},{4,5},{5,4},{6,7},{7,6},{8,9},{9,8},{10,11... | collective-permute-start | bytes 196616 | tf_op jit(solution)/shard_map/ppermute | solution.py:376
  539.6 89.6 %collective-permute-start.48 = (bf16[2,4,64,2048]{3,2,1,0:T(8,128)(2,1)S(1)}, bf16[2,4,64,2048]{3,2,1,0:T(8,128)(2,1)S(1)}, u32[]{:S(2)}, u32[]{:S(2)}) collective-permute-start(bf16[2,4,64,2048]{3,2,1,0:T(8,128)(2,1)S(1)} %dynamic-slice_bitcast_fusion.2), channel_id=1, source_target_pairs={{0,4},{2,6},{4,0},{6,2},{8,12},{10,14},{12,8},{14,10},{16,20},{18,... | collective-permute-start | bytes 6291464 | tf_op jit(solution)/shard_map/ppermute | solution.py:380
  543.1 85.4 %collective-permute-start.30 = (bf16[1,4,64,1536]{3,2,1,0:T(8,128)(2,1)S(1)}, bf16[1,4,64,1536]{3,2,1,0:T(8,128)(2,1)S(1)}, u32[]{:S(2)}, u32[]{:S(2)}) collective-permute-start(bf16[1,4,64,1536]{3,2,1,0:T(8,128)(2,1)S(1)} %dynamic-slice_bitcast_fusion.6), channel_id=1, source_target_pairs={{0,4},{2,6},{4,0},{6,2},{8,12},{10,14},{12,8},{14,10},{16,20},{18,... | collective-permute-start | bytes 2359304 | tf_op jit(solution)/shard_map/ppermute | solution.py:380
  628.8 14.2 %collective-permute-start.31 = (bf16[1,2,64,1536]{3,2,1,0:T(8,128)(2,1)S(1)}, bf16[1,2,64,1536]{3,2,1,0:T(8,128)(2,1)S(1)}, u32[]{:S(2)}, u32[]{:S(2)}) collective-permute-start(bf16[1,2,64,1536]{3,2,1,0:T(8,128)(2,1)S(1)} %dynamic-slice_bitcast_fusion.8), channel_id=1, source_target_pairs={{0,8},{2,10},{4,12},{6,14},{8,0},{10,2},{12,4},{14,6},{16,24},{18,... | collective-permute-start | bytes 1179656 | tf_op jit(solution)/shard_map/ppermute | solution.py:380
  630.3 42.9 %collective-permute-start.49 = (bf16[2,2,64,2048]{3,2,0,1:T(8,128)(2,1)S(1)}, bf16[2,2,64,2048]{3,2,0,1:T(8,128)(2,1)S(1)}, u32[]{:S(2)}, u32[]{:S(2)}) collective-permute-start(bf16[2,2,64,2048]{3,2,0,1:T(8,128)(2,1)S(1)} %bitcast.244), channel_id=1, source_target_pairs={{0,8},{2,10},{4,12},{6,14},{8,0},{10,2},{12,4},{14,6},{16,24},{18,... | collective-permute-start | bytes 3145736 | tf_op jit(solution)/shard_map/ppermute | solution.py:380
  634.7 61.2 %collective-permute-start.45 = (bf16[2,2,64,2048]{3,2,1,0:T(8,128)(2,1)S(1)}, bf16[2,2,64,2048]{3,2,1,0:T(8,128)(2,1)S(1)}, u32[]{:S(2)}, u32[]{:S(2)}) collective-permute-start(bf16[2,2,64,2048]{3,2,1,0:T(8,128)(2,1)S(1)} %dynamic-slice_bitcast_fusion.5), channel_id=1, source_target_pairs={{0,8},{2,10},{4,12},{6,14},{8,0},{10,2},{12,4},{14,6},{16,24},{18,... | collective-permute-start | bytes 3145736 | tf_op jit(solution)/shard_map/ppermute | solution.py:380
  643.1 72.4 %collective-permute-start.32 = (bf16[1,1,64,1536]{3,2,1,0:T(8,128)(2,1)S(1)}, bf16[1,1,64,1536]{3,2,1,0:T(8,128)(2,1)S(1)}, u32[]{:S(2)}, u32[]{:S(2)}) collective-permute-start(bf16[1,1,64,1536]{3,2,1,0:T(8,128)(2,1)S(1)} %constant_dynamic-slice_fusion.5), channel_id=1, source_target_pairs={{0,16},{2,18},{4,20},{6,22},{8,24},{10,26},{12,28},{14,30},{16,0},... | collective-permute-start | bytes 589832 | tf_op jit(solution)/shard_map/ppermute | solution.py:380
  673.6 37.8 %collective-permute-start.50 = (bf16[2,1,64,2048]{3,2,0,1:T(8,128)(2,1)S(1)}, bf16[2,1,64,2048]{3,2,0,1:T(8,128)(2,1)S(1)}, u32[]{:S(2)}, u32[]{:S(2)}) collective-permute-start(bf16[2,1,64,2048]{3,2,0,1:T(8,128)(2,1)S(1)} %constant_dynamic-slice_fusion), channel_id=1, source_target_pairs={{0,16},{2,18},{4,20},{6,22},{8,24},{10,26},{12,28},{14,30},{16,0},... | collective-permute-start | bytes 1572872 | tf_op jit(solution)/shard_map/ppermute | solution.py:380
  697.2 24.6 %collective-permute-start.46 = (bf16[2,1,64,2048]{3,2,1,0:T(8,128)(2,1)}, bf16[2,1,64,2048]{3,2,1,0:T(8,128)(2,1)}, u32[]{:S(2)}, u32[]{:S(2)}) collective-permute-start(bf16[2,1,64,2048]{3,2,1,0:T(8,128)(2,1)} %constant_dynamic-slice_fusion.3), channel_id=1, source_target_pairs={{0,16},{2,18},{4,20},{6,22},{8,24},{10,26},{12,28},{14,30},{16,0},... | collective-permute-start | bytes 1572872 | tf_op jit(solution)/shard_map/ppermute | solution.py:380
  711.6 10.3 %collective-permute-start.51 = (bf16[2,64,2048]{2,1,0:T(8,128)(2,1)S(1)}, bf16[2,64,2048]{2,1,0:T(8,128)(2,1)}, u32[]{:S(2)}, u32[]{:S(2)}) collective-permute-start(bf16[2,64,2048]{2,1,0:T(8,128)(2,1)S(1)} %fusion.41), channel_id=1, source_target_pairs={{0,1},{1,0},{2,3},{3,2},{4,5},{5,4},{6,7},{7,6},{8,9},{9,8},{10,11... | collective-permute-start | bytes 1572872 | tf_op jit(solution)/shard_map/ppermute | solution.py:376
  715.5 8.7 %copy-start.1 = (bf16[512,1024]{1,0:T(8,128)(2,1)S(1)}, bf16[512,1024]{1,0:T(8,128)(2,1)}, u32[]{:S(2)}) copy-start(bf16[512,1024]{1,0:T(8,128)(2,1)} %param.22) | copy-start | bytes 3145732
  (41 other events, 158.4 us)
